TPU v7x, 32 devices: a whole 2x2x4 slice. The times are simulated.
32 devices in a mesh: groups: 2 (over x), tensor: 8 (over z, y), section: 2 (over core).
Axes of the slice: x: 2, y: 2, z: 4, core: 2. Of those that a mesh axis runs over, the one named last changes fastest.
Arguments:
- prompt_states: bfloat16 [4, 512, 8192], P(('groups', 'section'), 'tensor'), parts along dimension 0
- decode_states: bfloat16 [4, 32, 8192], P(('groups', 'section'), 'tensor'), parts along dimension 0
- norm_gain: bfloat16 [8192], replicated, may hold values from 0.099609375 to 1.8984375
- w_query: bfloat16 [8192, 4096], P(None, 'tensor'), may hold values from -0.0625 to 0.0625
- w_keyvalue: bfloat16 [8192, 2048], P(None, 'tensor'), may hold values from -0.0625 to 0.0625
- w_output: bfloat16 [4096, 8192], P('tensor'), may hold values from -0.09375 to 0.09375
- cache_pages: bfloat16 [4, 512, 16, 2048], P(('groups', 'section'), 'tensor'), parts along dimension 0
- page_table: int32 [4, 32, 16], P(('groups', 'section'), 'tensor'), parts along dimension 0, may hold values from 0 to 63, as said below
- cache_len: int32 [4, 32], P(('groups', 'section')), parts along dimension 0, may hold values from 1 to 252, as said below
- dest_rank: int32 [4, 4], P('groups'), parts along dimension 0, may hold values from 0 to 7, as said below
- dest_page: int32 [4, 4, 8], P('groups'), parts along dimension 0, may hold values from 0 to 63, as said below
Outputs:
- layer_outputs: bfloat16 [4, 4, 32, 8192], P(None, ('groups', 'section'), 'tensor'), parts along dimension 1
There are 2 independent parts, one for each index of `groups`. A program takes and returns all parts, laid end to end along the dimension named above; an argument that names none is the same for every part. Nothing has to cross between parts.
Inputs may be any that keep to these rules, and one draw needn't show every extreme that they name: `page_table`: each device's table names each of its 64 local pages exactly once. `cache_len`: a request that receives a prompt has that prompt's length, 128 or fewer, and in each half one prompt has length 128; 252 is reached in every draw. `dest_rank`: distinct within a half. `dest_page`: the first 8 entries of the page table of one request of the receiving device.
All inputs are finite; a program needn't handle non-finite values.
Results may differ from a plain program's by a relative error of at most 0.03.
Values may be sent and summed in bfloat16 or wider, within the bound.
No kernel may reach another device: no remote copies, remote signals or barrier semaphores. Data moves between devices by JAX's collectives and lax.ppermute only.
A program may use at most 128 MiB of HBM per device.

v0:
```python
import functools

import jax
import jax.numpy as jnp
import numpy as np
from jax import lax
from jax.experimental import pallas as pl
from jax.experimental.pallas import tpu as pltpu
from jax.sharding import PartitionSpec as P

HD = 128
PLEN = 128
STEPS = 4
EPS = 1e-05
ROPE_BASE = 500000.0
LANES = 8
CHUNKS = 8
PAGE = 16
SURE = 16
MORE = (0, 8, 12, 16, 18, 20, 22, 24, 26, 28, 30, 32, 34, 36, 40)
VMEM_LIMIT = 10 * 1024 * 1024


def ring_shift(value, steps):
    count = lax.axis_size("tensor")
    return lax.ppermute(value, "tensor", [(s, (s + steps) % count) for s in range(count)])


def swap_xor(value, mask):
    count = lax.axis_size("tensor")
    return lax.ppermute(value, "tensor", [(s, s ^ mask) for s in range(count)])


def ring_arrivals(count):
    table, halves = [np.arange(count)] * 2, [0, 1]
    for hop in range(1, count // 2 + 1):
        for piece in range(2):
            for way in range(2):
                if hop < count // 2 or piece == way:
                    table.append((np.arange(count) - (1 - 2 * way) * hop) % count)
                    halves.append(piece)
    return np.stack(table, axis=1), halves


def along_ring(pieces, ready):
    count = lax.axis_size("tensor")
    blocks = list(pieces)
    going = [[rows, rows] for rows in pieces]
    for hop in range(1, count // 2 + 1):
        for piece in range(2):
            for way in range(2):
                if hop < count // 2 or piece == way:
                    going[piece][way] = ring_shift(going[piece][way], 1 - 2 * way)
                    blocks.append(going[piece][way])
        if hop == 1:
            going, ready = lax.optimization_barrier((going, ready))
    return [blocks[at : at + 8] for at in range(0, len(blocks), 8)], (), lambda pending: [], ready


def cross(value):
    return lax.ppermute(value, "tensor", [(r, r ^ 1) for r in range(8)])


def grid_arrivals():
    table = []
    for across in (0, 1):
        for origin in ((0, 1, 2, 3), (1, 0, 3, 2), (2, 2, 1, 1), (3, 3, 0, 0)):
            table.append(np.array([(2 * origin[r // 2] + r % 2) ^ across for r in range(8)]))
    return np.stack(table, axis=1), [0] * 8


def along_grid(pieces, ready):
    z = lax.axis_index("tensor") // 2

    def shift(rows, steps, starts):
        pairs = [(2 * s + c, 2 * (s + steps) + c) for s in starts for c in range(2)]
        return lax.ppermute(rows, "tensor", pairs)

    def pick(*rows):
        return jnp.where(z == 0, rows[0], jnp.where(z == 1, rows[1], jnp.where(z == 2, rows[2], rows[3])))

    (rows,) = pieces
    up, down = shift(rows, 1, (0, 1, 2)), shift(rows, -1, (1, 2, 3))
    up, down, parcels, weight = lax.optimization_barrier((up, down, *ready[:2]))
    section = lax.axis_index("section")
    half = weight.shape[0] // 2
    brought = cross(lax.dynamic_slice_in_dim(weight, section * half, half))
    ready = (parcels, *ready[2:])
    up2, down2 = shift(up, 1, (1, 2)), shift(down, -1, (1, 2))
    up2, down2, ready = lax.optimization_barrier((up2, down2, ready))
    outward = jnp.where(z == 1, down2, up2)
    ends = lax.ppermute(outward, "tensor", [(2, 0), (3, 1), (4, 6), (5, 7)])

    def finish(pending):
        up, down, up2, down2, ends, brought = pending
        given = lax.ppermute(brought, "section", [(0, 1), (1, 0)])
        begins = jnp.stack([section * half, (1 - section) * half]).astype(jnp.int32)
        second = pick(down, up, down, up)
        third = pick(down2, down, up, up2)
        fourth = pick(ends, down2, up2, ends)
        return [second, third, fourth], (brought, given), begins

    return [[rows]], (up, down, up2, down2, ends, brought), finish, ready


def rope_tables(positions, lib=jnp):
    half_dim = HD // 2
    freqs = ROPE_BASE ** (-(lib.arange(half_dim, dtype=lib.float32) * 2.0 / HD))
    angles = positions.astype(lib.float32)[:, None] * freqs[None, :].astype(lib.float32)
    cosine = lib.cos(angles)
    sine = lib.sin(angles)
    return (
        lib.concatenate([cosine, cosine], axis=1).astype(lib.float32),
        lib.concatenate([-sine, sine], axis=1).astype(lib.float32),
    )


def whole():
    return pl.BlockSpec(memory_space=pltpu.VMEM)


def normed_rows(values, gain):
    square = jnp.mean(values * values, axis=-1, keepdims=True)
    return values * lax.rsqrt(square + EPS) * gain


def prepare_kernel(prompt_ref, state_ref, gain_ref, *out_refs):
    tokens, width = prompt_ref.shape
    rows = tokens // len(out_refs)
    gain = gain_ref[...].astype(jnp.float32)
    for index, out_ref in enumerate(out_refs):
        part = prompt_ref[index * rows : (index + 1) * rows, :].astype(jnp.float32)
        out_ref[:rows, :] = normed_rows(part, gain).astype(jnp.bfloat16)
    states = normed_rows(state_ref[...].astype(jnp.float32), gain)
    filling = jnp.zeros((out_refs[-1].shape[0] - rows - states.shape[0], width), jnp.float32)
    out_refs[-1][rows:, :] = jnp.concatenate([states, filling], axis=0).astype(jnp.bfloat16)


def prepare(prompts, states, gain, pieces):
    tokens, width = prompts.shape
    rows = [tokens // pieces] * pieces
    rows[-1] += -(-states.shape[0] // LANES) * LANES
    return pl.pallas_call(
        prepare_kernel,
        out_shape=tuple(jax.ShapeDtypeStruct((count, width), jnp.bfloat16) for count in rows),
        in_specs=[whole()] * 3,
        out_specs=tuple(whole() for _ in rows),
        compiler_params=pltpu.CompilerParams(vmem_limit_bytes=VMEM_LIMIT),
        name="prepare",
    )(prompts, states, gain)


def prepare_blocks_kernel(prompt_in, state_in, gain_ref, out_ref, states, prompts, sems):
    each = state_in.shape[0]
    copies = [
        pltpu.make_async_copy(prompt_in, prompts, sems.at[0]),
        pltpu.make_async_copy(state_in, states, sems.at[1]),
    ]
    for copy in copies:
        copy.start()
    gain = gain_ref[...].astype(jnp.float32)
    lanes = gain.shape[1]
    for copy, rows_ref, first in zip(copies, (prompts, states), (0, prompts.shape[0] // each)):
        copy.wait()
        values = rows_ref[...].astype(jnp.float32)
        factor = lax.rsqrt(jnp.mean(values * values, axis=-1, keepdims=True) + EPS)
        for c in range(gain.shape[0]):
            part = slice(c * lanes, (c + 1) * lanes)
            normed = rows_ref[:, part].astype(jnp.float32) * factor * gain[c : c + 1, :]
            for block in range(rows_ref.shape[0] // each):
                rows = normed[block * each : (block + 1) * each, :]
                out_ref[first + block, :, part] = rows.astype(jnp.bfloat16)


def prepare_blocks(prompts, states, gain):
    tokens, width = prompts.shape
    each = states.shape[0]
    hbm = pl.BlockSpec(memory_space=pltpu.HBM)
    return pl.pallas_call(
        prepare_blocks_kernel,
        out_shape=(
            jax.ShapeDtypeStruct((tokens // each + 1, each, width), jnp.bfloat16),
            jax.ShapeDtypeStruct(states.shape, jnp.bfloat16),
        ),
        in_specs=[hbm, hbm, whole()],
        out_specs=(whole(), whole()),
        scratch_shapes=[
            pltpu.VMEM(prompts.shape, jnp.bfloat16),
            pltpu.SemaphoreType.DMA((2,)),
        ],
        compiler_params=pltpu.CompilerParams(vmem_limit_bytes=VMEM_LIMIT),
        name="prepare",
    )(
        pltpu.with_memory_space_constraint(prompts, pltpu.HBM),
        pltpu.with_memory_space_constraint(states, pltpu.HBM),
        gain,
    )


def project_kernel(rows, each, skipped, halves, *refs):
    heads = 2 if halves else 1
    blocks, refs = refs[: -7 - halves - heads], refs[-7 - halves - heads :]
    starts_ref, begins_ref, cos_ref, sin_ref = refs[:4]
    weight_ref, part_refs = refs[4], refs[5 : 5 + halves]
    out_refs = refs[5 + halves : 5 + halves + heads]
    states_ref, staged = refs[-2:]
    depth = weight_ref.shape[0] // CHUNKS

    def stage(span):
        for index, block in enumerate(blocks):
            begin = index * rows
            if block.ndim == 2:
                staged[begin : begin + rows, :] = block[:rows, span].astype(jnp.float32)
                continue
            for piece in range(rows // each):
                here = slice(begin + piece * each, begin + (piece + 1) * each)
                staged[here, :] = block[piece, :, span].astype(jnp.float32)
        return staged[...].astype(jnp.bfloat16)

    totals = [jnp.zeros(out_ref.shape, jnp.float32) for out_ref in out_refs]
    for c in range(CHUNKS):
        span = slice(c * depth, (c + 1) * depth)
        totals[0] += jnp.dot(stage(span), weight_ref[span, :], preferred_element_type=jnp.float32)
    for index, part_ref in enumerate(part_refs):
        for c in range(part_ref.shape[0] // depth):
            begin = pl.multiple_of(begins_ref[index] + c * depth, depth)
            totals[1] += jnp.dot(
                stage(pl.ds(begin, depth)),
                part_ref[c * depth : (c + 1) * depth, :],
                preferred_element_type=jnp.float32,
            )
    for total, out_ref in zip(totals, out_refs):
        out_ref[:, HD:] = total[:, HD:].astype(jnp.bfloat16)
        for index in range(len(blocks)):
            begin = starts_ref[skipped + index] % PLEN
            span = pl.ds(pl.multiple_of(begin, rows), rows)
            here = slice(index * rows, (index + 1) * rows)
            keys = turn(total[here, :HD], cos_ref[span, :], sin_ref[span, :])
            out_ref[here, :HD] = keys.astype(jnp.bfloat16)
    found = 0
    for block in blocks:
        if block.ndim == 3:
            states_ref[found] = block[rows // each]
            found += 1
        elif block.shape[0] > rows:
            states_ref[found] = block[rows:, :].astype(jnp.float32)[:each, :].astype(jnp.bfloat16)
            found += 1


def project(blocks, weight, starts, skipped, rows, each, parts=(), begins=None):
    width = weight.shape[0]
    cosine, sine = rope_tables(np.arange(PLEN), np)
    carrying = sum(block.ndim == 3 or block.shape[0] > rows for block in blocks)
    heads = 2 if parts else 1
    values = jax.ShapeDtypeStruct((len(blocks) * rows, 2 * HD), jnp.bfloat16)
    out_shape = [values] * heads
    out_shape.append(jax.ShapeDtypeStruct((carrying, each, width), jnp.bfloat16))
    smem = pl.BlockSpec(memory_space=pltpu.SMEM)
    begins = jnp.zeros((2,), jnp.int32) if begins is None else begins
    return pl.pallas_call(
        functools.partial(project_kernel, rows, each, skipped, len(parts)),
        out_shape=tuple(out_shape),
        in_specs=[whole()] * len(blocks) + [smem] * 2 + [whole()] * (3 + len(parts)),
        out_specs=tuple(whole() for _ in out_shape),
        scratch_shapes=[pltpu.VMEM((len(blocks) * rows, width // CHUNKS), jnp.float32)],
        compiler_params=pltpu.CompilerParams(vmem_limit_bytes=2 * VMEM_LIMIT),
        cost_estimate=pl.CostEstimate(
            flops=2 * len(blocks) * rows * weight.size * heads,
            bytes_accessed=2 * weight.size * heads,
            transcendentals=0,
        ),
        name="project",
    )(*blocks, starts, begins, cosine, sine, weight, *parts)


def parcels_kernel(heads, table_ref, used_ref, info_ref, pool_ref, sure_ref, more_ref, held, load_sem, store_sem):
    width = sure_ref.shape[-1]
    each, per_request = table_ref.shape
    pages = each * per_request
    sure = sure_ref.shape[1] - 1
    stores = []
    for target in range(len(heads)):
        copy = pltpu.make_async_copy(info_ref, sure_ref.at[target, 0], store_sem.at[0, target])
        copy.start()
        stores.append(copy)
    front = jnp.int32(0)
    back = used_ref[0]
    for r in range(1, each):
        back = back + used_ref[r]
    loads = []
    for r in range(each):
        used = used_ref[r]
        for p in range(per_request):
            spot = jnp.where(p < used, front + p, back + p - used)
            copy = pltpu.make_async_copy(
                pool_ref.at[table_ref[r, p]], held.at[spot], load_sem.at[r * per_request + p]
            )
            copy.start()
            loads.append(copy)
        front = front + used
        back = back + per_request - used
    for copy in loads:
        copy.wait()
    for target, head in enumerate(heads):
        columns = pl.ds(head * width, width)
        for bank, source, goal in (
            (1, held.at[pl.ds(0, sure), :, columns], sure_ref.at[target, pl.ds(1, sure)]),
            (2, held.at[pl.ds(sure, pages - sure), :, columns], more_ref.at[target]),
        ):
            copy = pltpu.make_async_copy(source, goal, store_sem.at[bank, target])
            copy.start()
            stores.append(copy)
    for copy in stores:
        copy.wait()


def make_parcels(table, used, info, pool, heads, width):
    pages, rows, _ = pool.shape
    hbm = pl.BlockSpec(memory_space=pltpu.HBM)
    smem = pl.BlockSpec(memory_space=pltpu.SMEM)
    return pl.pallas_call(
        functools.partial(parcels_kernel, heads),
        out_shape=(
            pltpu.HBM((len(heads), SURE + 1, rows, width), jnp.bfloat16),
            pltpu.HBM((len(heads), pages - SURE, rows, width), jnp.bfloat16),
        ),
        in_specs=[smem, smem, whole(), hbm],
        out_specs=(hbm, hbm),
        scratch_shapes=[
            pltpu.VMEM(pool.shape, jnp.bfloat16),
            pltpu.SemaphoreType.DMA((pages,)),
            pltpu.SemaphoreType.DMA((3, len(heads))),
        ],
        compiler_params=pltpu.CompilerParams(vmem_limit_bytes=VMEM_LIMIT),
        name="parcels",
    )(table, used, info, pltpu.with_memory_space_constraint(pool, pltpu.HBM))


def turn(values, cosine, sine):
    return values * cosine + pltpu.roll(values, HD // 2, 1) * sine


def step_kernel(blocks, iteration, groups, each, *refs):
    x_refs = refs[:blocks]
    order_ref, lens_ref, used_ref, first_ref, cos_ref, sin_ref = refs[blocks : blocks + 6]
    new_refs = refs[blocks + 6 : blocks + 6 + iteration]
    refs = refs[blocks + 6 + iteration :]
    if iteration == 0:
        target_ref, landing_ref, prompt_ref, offset_ref = refs[:4]
        arrived_refs = refs[4 : 4 + groups]
        refs = refs[4 + groups :]
        wq_in, wkv_in, wo_in, sure_in, more_in, out_ref, fresh_ref, wq, wkv, wo, cache = refs[:11]
        x_rows, q_s, score_s, mix_s, new_s, sems, patch_sems = refs[11:]
    else:
        wq, wkv, wo, cache = refs[:4]
        out_ref, fresh_ref, x_rows, q_s, score_s, mix_s, new_s = refs[4:]
    width, q_cols = wq.shape
    owners = cache.shape[0]
    count = owners * each
    span = (cache.shape[1] // PAGE - 1) // each * PAGE
    heads = q_cols // HD
    depth = width // CHUNKS

    waits = {}
    if iteration == 0:
        for c in range(CHUNKS):
            part = pl.ds(c * depth, depth)
            waits[c] = [
                pltpu.make_async_copy(wq_in.at[part, :], wq.at[part, :], sems.at[0, c]),
                pltpu.make_async_copy(wkv_in.at[part, :], wkv.at[part, :], sems.at[1, c]),
            ]
            waits["out", c] = [pltpu.make_async_copy(wo_in.at[:, part], wo.at[:, part], sems.at[2, c])]
        sure = sure_in.shape[1]
        waits["cache"] = [
            pltpu.make_async_copy(sure_in, cache.at[:, pl.ds(0, sure), :], sems.at[3, 0]),
            pltpu.make_async_copy(
                more_in, cache.at[:, pl.ds(sure, more_in.shape[1]), :], sems.at[3, 1]
            ),
        ]
        for name in [0, 1, 2, 3, "cache", 4, 5, 6, 7]:
            for copy in waits[name]:
                copy.start()

    def wait(name):
        for copy in waits.get(name, ()):
            copy.wait()

    def receivers():
        lines = [
            cache[owner, :PAGE, :HD].astype(jnp.float32)[:1, :] for owner in range(owners)
        ]
        firsts = jnp.concatenate(lines, axis=0)
        owner = lax.broadcasted_iota(jnp.int32, firsts.shape, 0)
        slot = lax.broadcasted_iota(jnp.int32, firsts.shape, 1)
        numbers = (owner * each + slot).astype(jnp.float32)
        found = []
        for k in range(target_ref.shape[0]):
            here = (owner == target_ref[k]) & (slot < each)
            here = here & (firsts == landing_ref[k].astype(jnp.float32))
            found.append(jnp.sum(jnp.where(here, numbers, 0.0)).astype(jnp.int32))
        return found

    def window(r, size, page=0):
        return pl.ds(pl.multiple_of((first_ref[r] + page + 1) * PAGE, PAGE), size)

    def patch(requests, action):
        pieces = offset_ref.shape[0]
        rows = sum(ref.shape[0] for ref in arrived_refs) // pieces
        piece = 0
        for ref in arrived_refs:
            for local in range(ref.shape[0] // rows):
                request = jnp.int32(0)
                for k, number in enumerate(requests):
                    request = jnp.where(prompt_ref[piece] == k, number, request)
                for p in range(rows // PAGE):
                    page = offset_ref[piece] // PAGE + p

                    @pl.when(page < used_ref[request])
                    def _():
                        copy = pltpu.make_async_copy(
                            ref.at[pl.ds(local * rows + p * PAGE, PAGE), :],
                            cache.at[request // each, window(request, PAGE, page), :],
                            patch_sems.at[piece, p],
                        )
                        action(copy)

                piece += 1

    place = 0
    for ref in x_refs:
        for rows in [ref[...]] if ref.ndim == 2 else [ref[k] for k in range(ref.shape[0])]:
            x_rows[place : place + each, :] = rows.astype(jnp.float32)
            place += each
    order = order_ref[...]

    query = jnp.zeros((count, q_cols), jnp.float32)
    keyvalue = jnp.zeros((count, 2 * HD), jnp.float32)
    for c in range(CHUNKS):
        part = slice(c * depth, (c + 1) * depth)
        x = jnp.dot(
            order, x_rows[:, part].astype(jnp.bfloat16), preferred_element_type=jnp.float32
        ).astype(jnp.bfloat16)
        wait(c)
        if iteration == 0:
            for copy in waits["out", c]:
                copy.start()
        query += jnp.dot(x, wq[part, :], preferred_element_type=jnp.float32)
        keyvalue += jnp.dot(x, wkv[part, :], preferred_element_type=jnp.float32)
        if iteration == 0 and c == CHUNKS - 2:
            wait("cache")
            requests = receivers()
            patch(requests, lambda copy: copy.start())

    cosine = cos_ref[iteration]
    sine = sin_ref[iteration]
    key = turn(keyvalue[:, :HD], cosine, sine).astype(jnp.bfloat16)
    value = keyvalue[:, HD:].astype(jnp.bfloat16)
    fresh_ref[:, :HD] = key
    fresh_ref[:, HD:] = value
    news = [(ref[:, :HD], ref[:, HD:]) for ref in new_refs] + [(key, value)]
    for j in range(LANES):
        lane = pl.ds(j, count, LANES)
        if j < heads:
            turned = turn(query[:, j * HD : (j + 1) * HD], cosine, sine).astype(jnp.bfloat16)
            q_s[lane, :] = turned.astype(jnp.float32)
        else:
            q_s[lane, :] = jnp.zeros((count, HD), jnp.float32)
        for t, pair in enumerate(news):
            for half in range(2):
                new_s[t, half, lane, :] = pair[half].astype(jnp.float32)

    if iteration == 0:
        patch(requests, lambda copy: copy.wait())
    scale = HD**-0.5
    column = lax.broadcasted_iota(jnp.int32, (LANES, span), 1)
    for r in range(count):
        rows = slice(r * LANES, (r + 1) * LANES)
        found = lax.dot_general(
            q_s[rows, :].astype(jnp.bfloat16),
            cache[r // each, window(r, span), :HD],
            (((1,), (1,)), ((), ())),
            preferred_element_type=jnp.float32,
        )
        score_s[rows, :] = jnp.where(column < lens_ref[r], found * scale, -1e30)

    scores = score_s[...]
    queries = q_s[...]
    fresh_scores = [
        jnp.sum(queries * new_s[t, 0], axis=-1, keepdims=True) * scale for t in range(iteration + 1)
    ]
    top = jnp.max(scores, axis=-1, keepdims=True)
    for s in fresh_scores:
        top = jnp.maximum(top, s)
    weights = jnp.exp(scores - top)
    fresh_weights = [jnp.exp(s - top) for s in fresh_scores]
    total = jnp.sum(weights, axis=-1, keepdims=True)
    for w in fresh_weights:
        total = total + w
    score_s[...] = weights / total
    row = lax.broadcasted_iota(jnp.int32, (span, HD), 0)
    for r in range(count):
        rows = slice(r * LANES, (r + 1) * LANES)
        mix_s[rows, :] = jnp.dot(
            score_s[rows, :].astype(jnp.bfloat16),
            jnp.where(
                row < lens_ref[r],
                cache[r // each, window(r, span), HD:],
                jnp.zeros((), jnp.bfloat16),
            ),
            preferred_element_type=jnp.float32,
        )
    mixed = mix_s[...]
    for t in range(iteration + 1):
        weight = (fresh_weights[t] / total).astype(jnp.bfloat16).astype(jnp.float32)
        mixed = mixed + weight * new_s[t, 1]
    mix_s[...] = mixed
    columns = jnp.concatenate(
        [mix_s[pl.ds(j, count, LANES), :].astype(jnp.bfloat16) for j in range(heads)], axis=1
    )
    for c in range(CHUNKS):
        part = slice(c * depth, (c + 1) * depth)
        wait(("out", c))
        product = jnp.dot(columns, wo[:, part], preferred_element_type=jnp.float32)
        for d in range(owners):
            out_ref[d, :, part] = product[d * each : (d + 1) * each, :].astype(jnp.bfloat16)


def step(x_blocks, order, lengths, used, first, cosine, sine, earlier, held, each, prompts=()):
    width, q_cols = held[0].shape
    owners = held[3].shape[0]
    count = owners * each
    cached = sum(a.shape[1] for a in held[3:])
    span = (cached // PAGE - 1) // each * PAGE
    iteration = len(earlier)
    blocks = len(x_blocks)
    groups = max(len(prompts) - 4, 0)
    smem = pl.BlockSpec(memory_space=pltpu.SMEM)
    hbm = pl.BlockSpec(memory_space=pltpu.HBM)
    anywhere = pl.BlockSpec(memory_space=pl.ANY)
    out_shape = [
        jax.ShapeDtypeStruct((owners, each, width), jnp.bfloat16),
        jax.ShapeDtypeStruct((count, 2 * HD), jnp.bfloat16),
    ]
    in_specs = [whole()] * (blocks + 1) + [smem] * 3 + [whole()] * (2 + iteration)
    scratch = [
        pltpu.VMEM((count, width), jnp.float32),
        pltpu.VMEM((count * LANES, HD), jnp.float32),
        pltpu.VMEM((count * LANES, span), jnp.float32),
        pltpu.VMEM((count * LANES, HD), jnp.float32),
        pltpu.VMEM((iteration + 1, 2, count * LANES, HD), jnp.float32),
    ]
    if iteration == 0:
        in_specs += [smem] * 4 + [whole()] * groups + [hbm] * 3 + [anywhere] * 2
        out_shape += [pltpu.VMEM(a.shape, a.dtype) for a in held[:3]]
        out_shape.append(pltpu.VMEM((owners, cached, 2 * HD), jnp.bfloat16))
        held = [pltpu.with_memory_space_constraint(a, pltpu.HBM) for a in held[:3]] + list(held[3:])
        pieces = prompts[3].shape[0]
        pages = sum(a.shape[0] for a in prompts[4:]) // pieces // PAGE
        scratch.append(pltpu.SemaphoreType.DMA((4, CHUNKS)))
        scratch.append(pltpu.SemaphoreType.DMA((pieces, pages)))
    else:
        in_specs += [whole()] * 4
    return pl.pallas_call(
        functools.partial(step_kernel, blocks, iteration, groups, each),
        out_shape=tuple(out_shape),
        in_specs=in_specs,
        out_specs=tuple(whole() for _ in out_shape),
        scratch_shapes=scratch,
        compiler_params=pltpu.CompilerParams(vmem_limit_bytes=VMEM_LIMIT),
        cost_estimate=pl.CostEstimate(
            flops=2 * count * width * (2 * q_cols + 2 * HD),
            bytes_accessed=2 * sum(a.size for a in held),
            transcendentals=count * LANES * span,
        ),
        name="decode_step",
    )(*x_blocks, order, lengths, used, first, cosine, sine, *earlier, *prompts, *held)


def settle_kernel(parts_ref, state_ref, gain_ref, next_ref, normed_ref):
    total = parts_ref[0].astype(jnp.float32)
    for d in range(1, parts_ref.shape[0]):
        total = total + parts_ref[d].astype(jnp.float32)
    state = (state_ref[...].astype(jnp.float32) + total).astype(jnp.bfloat16)
    next_ref[...] = state
    gain = gain_ref[...].astype(jnp.float32)
    normed_ref[...] = normed_rows(state.astype(jnp.float32), gain).astype(jnp.bfloat16)


def last_kernel(parts_ref, *refs):
    state_refs, out_ref = refs[:-1], refs[-1]
    total = parts_ref[0].astype(jnp.float32)
    for d in range(1, parts_ref.shape[0]):
        total = total + parts_ref[d].astype(jnp.float32)
    for index, state_ref in enumerate(state_refs):
        out_ref[index] = state_ref[...]
    out_ref[len(state_refs)] = (state_refs[-1][...].astype(jnp.float32) + total).astype(jnp.bfloat16)


def last(parts, states):
    return pl.pallas_call(
        last_kernel,
        out_shape=jax.ShapeDtypeStruct((len(states) + 1, *states[0].shape), jnp.bfloat16),
        in_specs=[whole()] * (1 + len(states)),
        out_specs=whole(),
        compiler_params=pltpu.CompilerParams(vmem_limit_bytes=VMEM_LIMIT),
        name="last",
    )(parts, *states)


def settle(parts, state, gain):
    shape = jax.ShapeDtypeStruct(state.shape, jnp.bfloat16)
    return pl.pallas_call(
        settle_kernel,
        out_shape=(shape, shape),
        in_specs=[whole()] * 3,
        out_specs=(whole(), whole()),
        compiler_params=pltpu.CompilerParams(vmem_limit_bytes=VMEM_LIMIT),
        name="settle",
    )(parts, state, gain)


def on_device(
    prompt_states,
    decode_states,
    norm_gain,
    w_query,
    w_keyvalue,
    w_output,
    cache_pages,
    page_table,
    cache_len,
    dest_rank,
    dest_page,
):
    rank = lax.axis_index("tensor")
    section = lax.axis_index("section")
    count = lax.axis_size("tensor")
    pool = cache_pages[0]
    page_size, kv_width = pool.shape[1:]
    own_table = page_table[0]
    lengths = cache_len[0]
    each, width = decode_states.shape[1:]
    tokens = prompt_states.shape[1]
    q_cols = w_query.shape[1]
    kv_heads = kv_width // (2 * HD)
    shared = count // kv_heads if count > kv_heads else 1
    gain = norm_gain[None, :]

    if w_keyvalue.shape[1] < 2 * HD:
        other = swap_xor(w_keyvalue, 1)
        is_key = rank % 2 == 0
        w_pair = jnp.concatenate(
            [jnp.where(is_key, w_keyvalue, other), jnp.where(is_key, other, w_keyvalue)], axis=1
        )
    else:
        w_pair = w_keyvalue

    sections = lax.axis_size("section")
    onward = [(s, (s + 1) % sections) for s in range(sections)]
    grid = count == 8 and sections == 2

    numbers = jnp.arange(count * each, dtype=jnp.int32)
    per_request = own_table.shape[1]
    used = (lengths + page_size - 1) // page_size
    by_owner = used.reshape(count, each)
    first = (jnp.cumsum(by_owner, axis=1) - by_owner).reshape(-1)
    most = jnp.max(jnp.sum(by_owner, axis=1, keepdims=True), keepdims=True)
    for axis in ("section", "groups"):
        for bit in range(lax.axis_size(axis).bit_length() - 1):
            pairs = [(s, s ^ (1 << bit)) for s in range(lax.axis_size(axis))]
            most = jnp.maximum(most, lax.ppermute(most, axis, pairs))
    own_used = lax.dynamic_slice_in_dim(used, rank * each, each)
    heads = tuple(target // shared for target in range(count))
    info = jnp.zeros((page_size, 2 * HD), jnp.bfloat16)
    info = info.at[0, :each].set(own_table[:, 0].astype(jnp.bfloat16))
    ready = make_parcels(own_table, own_used, info, pool, heads, 2 * HD)

    table, halves = grid_arrivals() if grid else ring_arrivals(count)
    parts = 1 if grid else 2
    rows = tokens // parts
    carried = np.array([index for index, piece in enumerate(halves) if piece == parts - 1])
    senders = jnp.asarray(table, jnp.int32)[rank]
    starts = senders * tokens + jnp.asarray(halves, jnp.int32) * rows
    orders = []
    masks = jnp.array([0, 1, 6, 4, 2, 7, 5, 3] if grid else range(count), jnp.int32)
    for owners in (senders[carried], rank ^ masks):
        rows_of = jnp.repeat(owners * each, each) + numbers % each
        orders.append((numbers[:, None] == rows_of[None, :]).astype(jnp.bfloat16))
    times = lengths[None, :] + jnp.arange(STEPS, dtype=jnp.int32)[:, None]
    cosine, sine = rope_tables(times.reshape(-1))
    cosine = cosine.reshape(STEPS, count * each, HD)
    sine = sine.reshape(STEPS, count * each, HD)
    sizes = [size for size in MORE if size < pool.shape[0] - SURE] + [pool.shape[0] - SURE]
    wanted = most[0, 0] - SURE
    choice = jnp.sum((wanted > jnp.array(sizes[:-1], jnp.int32)).astype(jnp.int32))
    ready = (ready, w_pair, choice, starts, orders, cosine, sine)
    if grid:
        lines = norm_gain.reshape(-1, HD)
        *pieces, state = prepare_blocks(prompt_states[0], decode_states[0], lines)
    else:
        state = decode_states[0]
        pieces = prepare(prompt_states[0], decode_states[0], gain, parts)
    known, pending, finish, ready = (along_grid if grid else along_ring)(pieces, ready)
    ready, *_, choice, starts, orders, cosine, sine = ready

    sure, more = ready

    def exchange(pages):
        return lax.all_to_all(
            pages.reshape(count, -1, 2 * HD), "tensor", split_axis=0, concat_axis=0, tiled=True
        )

    extra = more.shape[1]

    def branch(size):
        def run(more):
            if size == 0:
                return jnp.zeros((count, extra * page_size, 2 * HD), jnp.bfloat16)
            pages = exchange(more[:, :size])
            return jnp.pad(pages, ((0, 0), (0, (extra - size) * page_size), (0, 0)))

        return run

    more = lax.switch(choice, [branch(size) for size in sizes], more)
    known, pending, more = lax.optimization_barrier((known, pending, more))
    sure, _ = lax.optimization_barrier((sure, more))
    sure = exchange(sure)

    prompt_kv = []
    blocks = []
    if grid:
        rest, halves_of_other, begins = finish(pending)
        own, other, states = project(
            known[0] + rest, w_pair, starts, 0, rows, each, halves_of_other, begins
        )
        prompt_kv = [own, cross(other)]
        blocks = [states, cross(states)]
    else:
        skipped = 0
        for group in known:
            values, states = project(group, w_pair, starts, skipped, rows, each)
            prompt_kv.append(values)
            blocks.append(states)
            skipped += len(group)
    arrived = tuple(lax.ppermute(part, "section", onward) for part in prompt_kv)
    anchor = (section + 1) % sections
    targets = lax.dynamic_index_in_dim(dest_rank, anchor, 0, keepdims=False)
    landing = lax.dynamic_index_in_dim(dest_page, anchor, 0, keepdims=False)[:, 0]
    prompts = (targets, landing, starts // PLEN, starts % PLEN, *arrived)
    held = (w_query, w_pair, w_output, sure, more)

    blocks, cosine, sine, state, gain = lax.optimization_barrier((blocks, cosine, sine, state, gain))
    outputs = []
    earlier = []
    for iteration in range(STEPS):
        chosen = orders[min(iteration, 1)]
        parts, fresh, *fetched = step(
            blocks, chosen, lengths, used, first, cosine, sine, earlier, held, each, prompts
        )
        if iteration == 0:
            held, prompts = fetched, ()
        earlier.append(fresh)
        parts = lax.all_to_all(parts, "tensor", split_axis=0, concat_axis=0, tiled=True)
        if iteration + 1 < STEPS:
            state, normed = settle(parts, state, gain)
            outputs.append(state)
            if grid:
                along = [swap_xor(normed, bits) for bits in (6, 4, 2)]
                blocks = [normed, cross(normed), *along, *(cross(block) for block in along)]
            else:
                blocks = [normed] + [swap_xor(normed, bits) for bits in range(1, count)]
    return last(parts, outputs)[:, None]


def solution(mesh):
    in_specs = (
        P(("groups", "section"), "tensor", None),
        P(("groups", "section"), "tensor", None),
        P(),
        P(None, "tensor"),
        P(None, "tensor"),
        P("tensor", None),
        P(("groups", "section"), "tensor", None, None),
        P(("groups", "section"), "tensor", None),
        P(("groups", "section"), None),
        P("groups", None),
        P("groups", None, None),
    )
    out_specs = P(None, ("groups", "section"), "tensor", None)
    return jax.shard_map(
        on_device, mesh=mesh, in_specs=in_specs, out_specs=out_specs, check_vma=False
    )
```

profile of v0, /device:TPU:0, one launch (start us, length us, event | category | flops | bytes accessed | tf_op | source)
XLA Modules:
  0.0 294.8 jit_solution(10424282615298682136)
XLA Ops:
  0.7 2.3 prepare.1
  3.0 1.3 collective-permute-start.1
  4.3 6.6 %collective-permute-start = (bf16[17,4,8192]{2,1,0:T(4,128)(2,1)S(1)}, bf16[17,4,8192]{2,1,0:T(4,128)(2,1)}, u32[]{:S(2)}, u32[]{:S(2)}) collective-permute-start(bf16[17,4,8192]{2,1,0:T(4,128)(2,1)S(1)} %get-tuple-element.115.refs_0_), channel_id=1, source_target_pairs={{0,4},{2,6},{4,8},{6,10},{8,12},{10,14},{1,5},{3,7},{5,9},{7,11},{... | collective-permute-start | bytes 3342344 | tf_op jit(solution)/shard_map/ppermute | solution.py:77
  17.2 5.6 %parcels.1 = (bf16[8,17,16,256]{3,2,1,0:T(8,128)(2,1)}, bf16[8,48,16,256]{3,2,1,0:T(8,128)(2,1)}) custom-call(s32[4,16]{1,0:T(4,128)S(1)} %bitcast.47, s32[4]{0:T(128)S(1)} %dynamic_slice.17.used_ref, bf16[16,256]{1,0:T(8,128)(2,1)S(1)} %scatter.4.info_ref, bf16[64,16,2048]{2,1,0:T(8,128)(2,1)} %bitcast.62), custom_call_target="tpu_custom_call" | custom-call | tf_op jit(solution)/shard_map/parcels/pallas_call | solution.py:321
  23.3 9.2 %collective-permute-done.1 = bf16[17,4,8192]{2,1,0:T(4,128)(2,1)S(1)} collective-permute-done((bf16[17,4,8192]{2,1,0:T(4,128)(2,1)S(1)}, bf16[17,4,8192]{2,1,0:T(4,128)(2,1)S(1)}, u32[]{:S(2)}, u32[]{:S(2)}) %collective-permute-start.1) | collective-permute-done | bytes 1114144 | tf_op jit(solution)/shard_map/ppermute | solution.py:77
  32.5 1.2 collective-permute-done
  34.4 1.3 collective-permute-start.3
  37.8 3.0 %collective-permute-start.5 = (s32[1,1]{1,0:T(1,128)}, s32[1,1]{1,0:T(1,128)}, u32[]{:S(2)}, u32[]{:S(2)}) collective-permute-start(s32[1,1]{1,0:T(1,128)} %max.6), channel_id=1, source_target_pairs={{0,16},{16,0},{1,17},{17,1},{2,18},{18,2},{3,19},{19,3},{4,20},{20... | collective-permute-start | bytes 20 | tf_op jit(solution)/shard_map/ppermute | solution.py:671
  42.6 3.1 %constant_dynamic-slice_fusion.1 = bf16[4096,256]{1,0:T(8,128)(2,1)} fusion(bf16[8192,256]{1,0:T(8,128)(2,1)} %refs_15_.1, s32[]{:T(128)S(6)} %select_n.121), kind=kLoop, calls=%fused_computation.39 | loop fusion | bytes 4194308 | tf_op jit(solution)/shard_map/dynamic_slice | solution.py:87
  45.8 1.7 collective-permute-start.7
  47.5 17.8 %collective-permute-done.3 = bf16[17,4,8192]{2,1,0:T(4,128)(2,1)} collective-permute-done((bf16[17,4,8192]{2,1,0:T(4,128)(2,1)}, bf16[17,4,8192]{2,1,0:T(4,128)(2,1)}, u32[]{:S(2)}, u32[]{:S(2)}) %collective-permute-start.3) | collective-permute-done | bytes 1114144 | tf_op jit(solution)/shard_map/ppermute | solution.py:77
  65.3 1.6 broadcast_select_fusion
  66.9 1.3 collective-permute-start.6
  68.8 57.1 %conditional.1 = (bf16[8,768,256]{2,1,0:T(8,128)(2,1)}) conditional(s32[]{:T(128)} %clamp.3, () %tuple.64, bf16[8,48,16,256]{3,2,1,0:T(8,128)(2,1)} %get-tuple-element.114, bf16[8,48,16,256]{3,2,1,0:T(8,128)(2,1)} %get-tuple-element.114, bf16[8,48,16,256]{3,2,1,0:T(8,128)(2,1)} %get-tuple-element.114, ...), branch_computations={%region_3.4_spmd, %region_4.5_spmd, %region_5.6_spmd, %region_6.7_... | conditional | bytes 18874402 | solution.py:724
  68.8 1.5 slice-done.7
  70.3 53.6 %all_to_all.93 = bf16[8,448,256]{2,1,0:T(8,128)(2,1)S(1)} all-to-all(bf16[8,448,256]{2,1,0:T(8,128)(2,1)S(1)} %bitcast.56), channel_id=1, replica_groups=mesh['groups'=2,'tensor'=8,'section'=2] {'tensor'}, dimensions={0} | all-to-all | bytes 3670016 | tf_op jit(solution)/shard_map/cond/branch_9_fun/all_to_all | solution.py:709
  123.9 1.9 pad.55
  125.9 3.7 %all-to-all-start.15 = ((bf16[8,272,256]{2,1,0:T(8,128)(2,1)}), bf16[8,272,256]{2,1,0:T(8,128)(2,1)S(1)}, u32[]{:S(2)}, u32[]{:S(2)}) async-start(bf16[8,272,256]{2,1,0:T(8,128)(2,1)} %bitcast.64), calls=%async_computation.15 | async-start | bytes 2228224 | tf_op jit(solution)/shard_map/all_to_all | solution.py:709
  129.7 3.9 %select_select_fusion.1 = (bf16[17,4,8192]{2,1,0:T(4,128)(2,1)S(1)}, bf16[17,4,8192]{2,1,0:T(4,128)(2,1)S(1)}, bf16[17,4,8192]{2,1,0:T(4,128)(2,1)S(1)}) fusion(bf16[17,4,8192]{2,1,0:T(4,128)(2,1)} %collective-permute-done.6, bf16[17,4,8192]{2,1,0:T(4,128)(2,1)} %collective-permute-done.3, bf16[17,4,8192]{2,1,0:T(4,128)(2,1)} %copy-done.13, pred[]{:T(512)S(6)} %eq.57, ...), kind=kLoop, calls=%fused_computation.3 | loop fusion | flops 5013504 | bytes 8912899 | tf_op jit(solution)/shard_map/jit(_where)/select_n | solution.py:80
  133.9 7.4 %project.1 = (bf16[256,256]{1,0:T(8,128)(2,1)}, bf16[256,256]{1,0:T(8,128)(2,1)S(1)}, bf16[4,4,8192]{2,1,0:T(4,128)(2,1)S(1)}) custom-call(bf16[17,4,8192]{2,1,0:T(4,128)(2,1)S(1)} %copy-done.4, bf16[17,4,8192]{2,1,0:T(4,128)(2,1)S(1)} %get-tuple-element.163.refs_1_, bf16[17,4,8192]{2,1,0:T(4,128)(2,1)S(1)} %get-tuple-element.162.refs_2_, ...), custom_call_target="tpu_custom_call" | custom-call | flops 2147483648 | bytes 8388608 | tf_op jit(solution)/shard_map/project/pallas_call | solution.py:260
  141.2 2.0 collective-permute-start.11
  144.3 7.1 %collective-permute-done.11 = bf16[256,256]{1,0:T(8,128)(2,1)S(1)} collective-permute-done((bf16[256,256]{1,0:T(8,128)(2,1)S(1)}, bf16[256,256]{1,0:T(8,128)(2,1)S(1)}, u32[]{:S(2)}, u32[]{:S(2)}) %collective-permute-start.11) | collective-permute-done | bytes 131104 | tf_op jit(solution)/shard_map/ppermute | solution.py:61
  151.4 5.3 %collective-permute-done.9.refs_1_ = bf16[4,4,8192]{2,1,0:T(4,128)(2,1)S(1)} collective-permute-done((bf16[4,4,8192]{2,1,0:T(4,128)(2,1)S(1)}, bf16[4,4,8192]{2,1,0:T(4,128)(2,1)S(1)}, u32[]{:S(2)}, u32[]{:S(2)}) %collective-permute-start.9) | collective-permute-done | bytes 262176 | tf_op jit(solution)/shard_map/ppermute | solution.py:61
  158.7 12.5 %decode_step.4 = (bf16[8,4,8192]{2,1,0:T(4,128)(2,1)S(1)}, bf16[32,256]{1,0:T(8,128)(2,1)S(1)}, bf16[8192,512]{1,0:T(8,128)(2,1)S(1)}, bf16[8192,256]{1,0:T(8,12...) custom-call(bf16[4,4,8192]{2,1,0:T(4,128)(2,1)S(1)} %copy-done.6, ...), custom_call_target="tpu_custom_call" | custom-call | flops 671088640 | bytes 25231360 | tf_op jit(solution)/shard_map/decode_step/pallas_call | solution.py:563
  171.2 18.3 %all_to_all.100.parts_ref = bf16[8,4,8192]{2,1,0:T(4,128)(2,1)S(1)} all-to-all(bf16[8,4,8192]{2,1,0:T(4,128)(2,1)S(1)} %get-tuple-element.137), channel_id=1, replica_groups=mesh['groups'=2,'tensor'=8,'section'=2] {'tensor'}, dimensions={0} | all-to-all | bytes 1048576 | tf_op jit(solution)/shard_map/all_to_all | solution.py:763
  189.8 1.2 collective-permute-start.16
  191.6 2.7 collective-permute-start.14
  194.3 1.5 collective-permute-start.13
  197.8 1.7 collective-permute-start.17
  200.0 1.1 collective-permute-done.18.refs_6_
  202.0 6.2 %decode_step.5 = (bf16[8,4,8192]{2,1,0:T(4,128)(2,1)S(1)}, bf16[32,256]{1,0:T(8,128)(2,1)S(1)}) custom-call(bf16[4,8192]{1,0:T(4,128)(2,1)S(1)} %get-tuple-element.140.refs_0_, bf16[4,8192]{1,0:T(4,128)(2,1)S(1)} %collective-permute-done.13.refs_1_, bf16[4,8192]{1,0:T(4,128)(2,1)S(1)} %collective-permute-done.14.refs_2_, ...), custom_call_target="tpu_custom_call" | custom-call | flops 671088640 | bytes 25231360 | tf_op jit(solution)/shard_map/decode_step/pallas_call | solution.py:563
  208.2 15.9 %all_to_all.101.parts_ref = bf16[8,4,8192]{2,1,0:T(4,128)(2,1)S(1)} all-to-all(bf16[8,4,8192]{2,1,0:T(4,128)(2,1)S(1)} %get-tuple-element.147), channel_id=1, replica_groups=mesh['groups'=2,'tensor'=8,'section'=2] {'tensor'}, dimensions={0} | all-to-all | bytes 1048576 | tf_op jit(solution)/shard_map/all_to_all | solution.py:763
  224.4 1.2 collective-permute-start.23
  226.4 2.5 collective-permute-start.21
  228.9 1.5 collective-permute-start.20
  230.3 1.3 collective-permute-start.26
  232.5 1.5 collective-permute-start.24
  234.6 1.3 collective-permute-done.25.refs_6_
  236.8 6.2 %decode_step.6 = (bf16[8,4,8192]{2,1,0:T(4,128)(2,1)S(1)}, bf16[32,256]{1,0:T(8,128)(2,1)S(1)}) custom-call(bf16[4,8192]{1,0:T(4,128)(2,1)S(1)} %get-tuple-element.149.refs_0_, bf16[4,8192]{1,0:T(4,128)(2,1)S(1)} %collective-permute-done.20.refs_1_, bf16[4,8192]{1,0:T(4,128)(2,1)S(1)} %collective-permute-done.21.refs_2_, ...), custom_call_target="tpu_custom_call" | custom-call | flops 671088640 | bytes 25231360 | tf_op jit(solution)/shard_map/decode_step/pallas_call | solution.py:563
  243.0 16.7 %all_to_all.102.parts_ref = bf16[8,4,8192]{2,1,0:T(4,128)(2,1)S(1)} all-to-all(bf16[8,4,8192]{2,1,0:T(4,128)(2,1)S(1)} %get-tuple-element.151), channel_id=1, replica_groups=mesh['groups'=2,'tensor'=8,'section'=2] {'tensor'}, dimensions={0} | all-to-all | bytes 1048576 | tf_op jit(solution)/shard_map/all_to_all | solution.py:763
  260.5 2.3 collective-permute-start.29
  262.8 1.7 collective-permute-start.28
  264.5 1.6 collective-permute-start.27
  266.5 1.6 collective-permute-start.32
  268.9 1.8 collective-permute-start.31
  271.1 2.1 collective-permute-done.31.refs_5_
  273.1 6.3 %decode_step.7 = (bf16[8,4,8192]{2,1,0:T(4,128)(2,1)S(1)}, bf16[32,256]{1,0:T(8,128)(2,1)}) custom-call(bf16[4,8192]{1,0:T(4,128)(2,1)S(1)} %get-tuple-element.153.refs_0_, bf16[4,8192]{1,0:T(4,128)(2,1)S(1)} %collective-permute-done.27.refs_1_, bf16[4,8192]{1,0:T(4,128)(2,1)S(1)} %collective-permute-done.28.refs_2_, ...), custom_call_target="tpu_custom_call" | custom-call | flops 671088640 | bytes 25231360 | tf_op jit(solution)/shard_map/decode_step/pallas_call | solution.py:563
  279.4 14.1 %all_to_all.103.parts_ref = bf16[8,4,8192]{2,1,0:T(4,128)(2,1)S(1)} all-to-all(bf16[8,4,8192]{2,1,0:T(4,128)(2,1)S(1)} %get-tuple-element.155), channel_id=1, replica_groups=mesh['groups'=2,'tensor'=8,'section'=2] {'tensor'}, dimensions={0} | all-to-all | bytes 1048576 | tf_op jit(solution)/shard_map/all_to_all | solution.py:763
  (115 shorter events, 24.3 us)
Async XLA Ops:
  0.0 68.2 %copy-start = (s32[2,4,8]{2,1,0:T(4,128)S(1)}, s32[2,4,8]{2,1,0:T(4,128)}, u32[]{:S(2)}) copy-start(s32[2,4,8]{2,1,0:T(4,128)} %param.47) | copy-start | bytes 772
  3.0 19.8 %copy-start.3 = (bf16[17,4,8192]{2,1,0:T(4,128)(2,1)}, bf16[17,4,8192]{2,1,0:T(4,128)(2,1)S(1)}, u32[]{:S(2)}) copy-start(bf16[17,4,8192]{2,1,0:T(4,128)(2,1)S(1)} %get-tuple-element.115.refs_0_) | copy-start | bytes 3342340
  3.0 29.5 %collective-permute-start.1 = (bf16[17,4,8192]{2,1,0:T(4,128)(2,1)S(1)}, bf16[17,4,8192]{2,1,0:T(4,128)(2,1)S(1)}, u32[]{:S(2)}, u32[]{:S(2)}) collective-permute-start(bf16[17,4,8192]{2,1,0:T(4,128)(2,1)S(1)} %get-tuple-element.115.refs_0_), channel_id=1, source_target_pairs={{4,0},{6,2},{8,4},{10,6},{12,8},{14,10},{5,1},{7,3},{9,5},{11,7},{... | collective-permute-start | bytes 3342344 | tf_op jit(solution)/shard_map/ppermute | solution.py:77
  4.3 29.4 %collective-permute-start = (bf16[17,4,8192]{2,1,0:T(4,128)(2,1)S(1)}, bf16[17,4,8192]{2,1,0:T(4,128)(2,1)}, u32[]{:S(2)}, u32[]{:S(2)}) collective-permute-start(bf16[17,4,8192]{2,1,0:T(4,128)(2,1)S(1)} %get-tuple-element.115.refs_0_), channel_id=1, source_target_pairs={{0,4},{2,6},{4,8},{6,10},{8,12},{10,14},{1,5},{3,7},{5,9},{7,11},{... | collective-permute-start | bytes 3342344 | tf_op jit(solution)/shard_map/ppermute | solution.py:77
  12.4 24.0 %collective-permute-start.4 = (s32[1,1]{1,0:T(1,128)}, s32[1,1]{1,0:T(1,128)}, u32[]{:S(2)}, u32[]{:S(2)}) collective-permute-start(s32[1,1]{1,0:T(1,128)} %bitcast.21), channel_id=1, source_target_pairs={{0,1},{1,0},{2,3},{3,2},{4,5},{5,4},{6,7},{7,6},{8,9},{9,8},{10,11... | collective-permute-start | bytes 20 | tf_op jit(solution)/shard_map/ppermute | solution.py:671
  17.2 5.6 %copy-start.11 = (s32[1,32]{1,0:T(1,128)S(1)}, s32[1,32]{1,0:T(1,128)}, u32[]{:S(2)}) copy-start(s32[1,32]{1,0:T(1,128)} %param.45) | copy-start | bytes 388
  17.2 24.8 %copy-start.16 = (s32[15]{0:T(128)S(1)}, s32[15]{0:T(128)}, u32[]{:S(2)}) copy-start(s32[15]{0:T(128)} %constant.222.clone) | copy-start | bytes 184
  33.7 13.8 %collective-permute-start.2 = (bf16[17,4,8192]{2,1,0:T(4,128)(2,1)}, bf16[17,4,8192]{2,1,0:T(4,128)(2,1)S(1)}, u32[]{:S(2)}, u32[]{:S(2)}) collective-permute-start(bf16[17,4,8192]{2,1,0:T(4,128)(2,1)} %collective-permute-done), channel_id=1, source_target_pairs={{4,8},{6,10},{8,12},{10,14},{5,9},{7,11},{9,13},{11,15},{20,24},{2... | collective-permute-start | bytes 3342344 | tf_op jit(solution)/shard_map/ppermute | solution.py:77
  34.4 30.9 %collective-permute-start.3 = (bf16[17,4,8192]{2,1,0:T(4,128)(2,1)}, bf16[17,4,8192]{2,1,0:T(4,128)(2,1)}, u32[]{:S(2)}, u32[]{:S(2)}) collective-permute-start(bf16[17,4,8192]{2,1,0:T(4,128)(2,1)} %copy-done.14), channel_id=1, source_target_pairs={{4,0},{6,2},{8,4},{10,6},{5,1},{7,3},{9,5},{11,7},{20,16},{22,18},... | collective-permute-start | bytes 3342344 | tf_op jit(solution)/shard_map/ppermute | solution.py:77
  37.8 3.6 %collective-permute-start.5 = (s32[1,1]{1,0:T(1,128)}, s32[1,1]{1,0:T(1,128)}, u32[]{:S(2)}, u32[]{:S(2)}) collective-permute-start(s32[1,1]{1,0:T(1,128)} %max.6), channel_id=1, source_target_pairs={{0,16},{16,0},{1,17},{17,1},{2,18},{18,2},{3,19},{19,3},{4,20},{20... | collective-permute-start | bytes 20 | tf_op jit(solution)/shard_map/ppermute | solution.py:671
  45.8 80.1 %collective-permute-start.7 = (bf16[4096,256]{1,0:T(8,128)(2,1)}, bf16[4096,256]{1,0:T(8,128)(2,1)S(1)}, u32[]{:S(2)}, u32[]{:S(2)}) collective-permute-start(bf16[4096,256]{1,0:T(8,128)(2,1)} %constant_dynamic-slice_fusion.1), channel_id=1, source_target_pairs={{0,2},{2,0},{4,6},{6,4},{8,10},{10,8},{12,14},{14,12},{1,3},{3,1},... | collective-permute-start | bytes 6291464 | tf_op jit(solution)/shard_map/ppermute | solution.py:61
  47.4 21.3 %copy-start.13 = (bf16[17,4,8192]{2,1,0:T(4,128)(2,1)}, bf16[17,4,8192]{2,1,0:T(4,128)(2,1)S(1)}, u32[]{:S(2)}) copy-start(bf16[17,4,8192]{2,1,0:T(4,128)(2,1)S(1)} %collective-permute-done.2) | copy-start | bytes 3342340
  66.9 59.0 %collective-permute-start.6 = (bf16[17,4,8192]{2,1,0:T(4,128)(2,1)}, bf16[17,4,8192]{2,1,0:T(4,128)(2,1)}, u32[]{:S(2)}, u32[]{:S(2)}) collective-permute-start(bf16[17,4,8192]{2,1,0:T(4,128)(2,1)} %broadcast_select_fusion), channel_id=1, source_target_pairs={{4,0},{6,2},{8,12},{10,14},{5,1},{7,3},{9,13},{11,15},{20,16},{22,... | collective-permute-start | bytes 3342344 | tf_op jit(solution)/shard_map/ppermute | solution.py:92
  68.8 1.5 slice-start.7
  125.9 7.8 %collective-permute-start.8 = (bf16[4096,256]{1,0:T(8,128)(2,1)S(1)}, bf16[4096,256]{1,0:T(8,128)(2,1)}, u32[]{:S(2)}, u32[]{:S(2)}) collective-permute-start(bf16[4096,256]{1,0:T(8,128)(2,1)S(1)} %collective-permute-done.7.refs_9_), channel_id=1, source_target_pairs={{0,1},{1,0},{2,3},{3,2},{4,5},{5,4},{6,7},{7,6},{8,9},{9,8},{10,11... | collective-permute-start | bytes 6291464 | tf_op jit(solution)/shard_map/ppermute | solution.py:96
  125.9 31.8 %all-to-all-start.15 = ((bf16[8,272,256]{2,1,0:T(8,128)(2,1)}), bf16[8,272,256]{2,1,0:T(8,128)(2,1)S(1)}, u32[]{:S(2)}, u32[]{:S(2)}) async-start(bf16[8,272,256]{2,1,0:T(8,128)(2,1)} %bitcast.64), calls=%async_computation.15 | async-start | bytes 2228224 | tf_op jit(solution)/shard_map/all_to_all | solution.py:709
  129.7 4.0 %copy-start.2 = (bf16[8192,256]{1,0:T(8,128)(2,1)S(1)}, bf16[8192,256]{1,0:T(8,128)(2,1)}, u32[]{:S(2)}) copy-start(bf16[8192,256]{1,0:T(8,128)(2,1)} %refs_15_.1) | copy-start | bytes 12582916
  129.7 4.2 %copy-start.4 = (bf16[17,4,8192]{2,1,0:T(4,128)(2,1)S(1)}, bf16[17,4,8192]{2,1,0:T(4,128)(2,1)}, u32[]{:S(2)}) copy-start(bf16[17,4,8192]{2,1,0:T(4,128)(2,1)} %copy-done.3) | copy-start | bytes 3342340
  129.7 4.2 %copy-start.7 = (f32[128,128]{1,0:T(8,128)S(1)}, f32[128,128]{1,0:T(8,128)}, u32[]{:S(2)}) copy-start(f32[128,128]{1,0:T(8,128)} %constant.224.clone.refs_7_) | copy-start | bytes 196612
  129.7 4.2 %copy-start.8 = (f32[128,128]{1,0:T(8,128)S(1)}, f32[128,128]{1,0:T(8,128)}, u32[]{:S(2)}) copy-start(f32[128,128]{1,0:T(8,128)} %constant.223.clone.refs_6_) | copy-start | bytes 196612
  133.9 10.3 %copy-start.15 = (s32[2,4]{1,0:T(2,128)S(1)}, s32[2,4]{1,0:T(2,128)}, u32[]{:S(2)}) copy-start(s32[2,4]{1,0:T(2,128)} %param.46) | copy-start | bytes 100
  133.9 10.3 %copy-start.10 = (bf16[8192]{0:T(1024)(128)(2,1)S(1)}, bf16[8192]{0:T(1024)(128)(2,1)}, u32[]{:S(2)}) copy-start(bf16[8192]{0:T(1024)(128)(2,1)} %param.39) | copy-start | bytes 49156
  141.2 10.2 %collective-permute-start.11 = (bf16[256,256]{1,0:T(8,128)(2,1)S(1)}, bf16[256,256]{1,0:T(8,128)(2,1)S(1)}, u32[]{:S(2)}, u32[]{:S(2)}) collective-permute-start(bf16[256,256]{1,0:T(8,128)(2,1)S(1)} %get-tuple-element.133), channel_id=1, source_target_pairs={{0,2},{2,0},{4,6},{6,4},{8,10},{10,8},{12,14},{14,12},{1,3},{3,1},... | collective-permute-start | bytes 393224 | tf_op jit(solution)/shard_map/ppermute | solution.py:61
  143.3 13.4 %collective-permute-start.9 = (bf16[4,4,8192]{2,1,0:T(4,128)(2,1)S(1)}, bf16[4,4,8192]{2,1,0:T(4,128)(2,1)S(1)}, u32[]{:S(2)}, u32[]{:S(2)}) collective-permute-start(bf16[4,4,8192]{2,1,0:T(4,128)(2,1)S(1)} %get-tuple-element.127.refs_0_), channel_id=1, source_target_pairs={{0,2},{2,0},{4,6},{6,4},{8,10},{10,8},{12,14},{14,12},{1,3},{3,1},... | collective-permute-start | bytes 786440 | tf_op jit(solution)/shard_map/ppermute | solution.py:61
  144.2 13.6 %collective-permute-start.10 = (bf16[256,256]{1,0:T(8,128)(2,1)}, bf16[256,256]{1,0:T(8,128)(2,1)S(1)}, u32[]{:S(2)}, u32[]{:S(2)}) collective-permute-start(bf16[256,256]{1,0:T(8,128)(2,1)} %get-tuple-element.132), channel_id=1, source_target_pairs={{0,1},{1,0},{2,3},{3,2},{4,5},{5,4},{6,7},{7,6},{8,9},{9,8},{10,11... | collective-permute-start | bytes 393224 | tf_op jit(solution)/shard_map/ppermute | solution.py:745
  151.4 6.4 %collective-permute-start.12 = (bf16[256,256]{1,0:T(8,128)(2,1)S(1)}, bf16[256,256]{1,0:T(8,128)(2,1)S(1)}, u32[]{:S(2)}, u32[]{:S(2)}) collective-permute-start(bf16[256,256]{1,0:T(8,128)(2,1)S(1)} %collective-permute-done.11), channel_id=1, source_target_pairs={{0,1},{1,0},{2,3},{3,2},{4,5},{5,4},{6,7},{7,6},{8,9},{9,8},{10,11... | collective-permute-start | bytes 393224 | tf_op jit(solution)/shard_map/ppermute | solution.py:745
  189.8 5.9 %collective-permute-start.16 = (bf16[4,8192]{1,0:T(4,128)(2,1)S(1)}, bf16[4,8192]{1,0:T(4,128)(2,1)S(1)}, u32[]{:S(2)}, u32[]{:S(2)}) collective-permute-start(bf16[4,8192]{1,0:T(4,128)(2,1)S(1)} %get-tuple-element.140.refs_0_), channel_id=1, source_target_pairs={{0,4},{2,6},{4,0},{6,2},{8,12},{10,14},{12,8},{14,10},{1,5},{3,7},... | collective-permute-start | bytes 196616 | tf_op jit(solution)/shard_map/ppermute | solution.py:31
  191.0 5.9 %collective-permute-start.15 = (bf16[4,8192]{1,0:T(4,128)(2,1)S(1)}, bf16[4,8192]{1,0:T(4,128)(2,1)S(1)}, u32[]{:S(2)}, u32[]{:S(2)}) collective-permute-start(bf16[4,8192]{1,0:T(4,128)(2,1)S(1)} %get-tuple-element.140.refs_0_), channel_id=1, source_target_pairs={{0,8},{2,10},{4,12},{6,14},{8,0},{10,2},{12,4},{14,6},{1,9},{3,11}... | collective-permute-start | bytes 196616 | tf_op jit(solution)/shard_map/ppermute | solution.py:31
  191.6 6.2 %collective-permute-start.14 = (bf16[4,8192]{1,0:T(4,128)(2,1)S(1)}, bf16[4,8192]{1,0:T(4,128)(2,1)S(1)}, u32[]{:S(2)}, u32[]{:S(2)}) collective-permute-start(bf16[4,8192]{1,0:T(4,128)(2,1)S(1)} %get-tuple-element.140.refs_0_), channel_id=1, source_target_pairs={{0,12},{2,14},{4,8},{6,10},{8,4},{10,6},{12,0},{14,2},{1,13},{3,15... | collective-permute-start | bytes 196616 | tf_op jit(solution)/shard_map/ppermute | solution.py:31
  194.3 5.2 %collective-permute-start.13 = (bf16[4,8192]{1,0:T(4,128)(2,1)S(1)}, bf16[4,8192]{1,0:T(4,128)(2,1)S(1)}, u32[]{:S(2)}, u32[]{:S(2)}) collective-permute-start(bf16[4,8192]{1,0:T(4,128)(2,1)S(1)} %get-tuple-element.140.refs_0_), channel_id=1, source_target_pairs={{0,2},{2,0},{4,6},{6,4},{8,10},{10,8},{12,14},{14,12},{1,3},{3,1},... | collective-permute-start | bytes 196616 | tf_op jit(solution)/shard_map/ppermute | solution.py:61
  195.7 4.3 %collective-permute-start.19 = (bf16[4,8192]{1,0:T(4,128)(2,1)S(1)}, bf16[4,8192]{1,0:T(4,128)(2,1)S(1)}, u32[]{:S(2)}, u32[]{:S(2)}) collective-permute-start(bf16[4,8192]{1,0:T(4,128)(2,1)S(1)} %collective-permute-done.16.refs_4_), channel_id=1, source_target_pairs={{0,2},{2,0},{4,6},{6,4},{8,10},{10,8},{12,14},{14,12},{1,3},{3,1},... | collective-permute-start | bytes 196616 | tf_op jit(solution)/shard_map/ppermute | solution.py:61
  196.9 4.3 %collective-permute-start.18 = (bf16[4,8192]{1,0:T(4,128)(2,1)S(1)}, bf16[4,8192]{1,0:T(4,128)(2,1)S(1)}, u32[]{:S(2)}, u32[]{:S(2)}) collective-permute-start(bf16[4,8192]{1,0:T(4,128)(2,1)S(1)} %collective-permute-done.15.refs_3_), channel_id=1, source_target_pairs={{0,2},{2,0},{4,6},{6,4},{8,10},{10,8},{12,14},{14,12},{1,3},{3,1},... | collective-permute-start | bytes 196616 | tf_op jit(solution)/shard_map/ppermute | solution.py:61
  197.8 4.3 %collective-permute-start.17 = (bf16[4,8192]{1,0:T(4,128)(2,1)S(1)}, bf16[4,8192]{1,0:T(4,128)(2,1)S(1)}, u32[]{:S(2)}, u32[]{:S(2)}) collective-permute-start(bf16[4,8192]{1,0:T(4,128)(2,1)S(1)} %collective-permute-done.14.refs_2_), channel_id=1, source_target_pairs={{0,2},{2,0},{4,6},{6,4},{8,10},{10,8},{12,14},{14,12},{1,3},{3,1},... | collective-permute-start | bytes 196616 | tf_op jit(solution)/shard_map/ppermute | solution.py:61
  224.4 5.9 %collective-permute-start.23 = (bf16[4,8192]{1,0:T(4,128)(2,1)S(1)}, bf16[4,8192]{1,0:T(4,128)(2,1)S(1)}, u32[]{:S(2)}, u32[]{:S(2)}) collective-permute-start(bf16[4,8192]{1,0:T(4,128)(2,1)S(1)} %get-tuple-element.149.refs_0_), channel_id=1, source_target_pairs={{0,4},{2,6},{4,0},{6,2},{8,12},{10,14},{12,8},{14,10},{1,5},{3,7},... | collective-permute-start | bytes 196616 | tf_op jit(solution)/shard_map/ppermute | solution.py:31
  225.6 6.0 %collective-permute-start.22 = (bf16[4,8192]{1,0:T(4,128)(2,1)S(1)}, bf16[4,8192]{1,0:T(4,128)(2,1)S(1)}, u32[]{:S(2)}, u32[]{:S(2)}) collective-permute-start(bf16[4,8192]{1,0:T(4,128)(2,1)S(1)} %get-tuple-element.149.refs_0_), channel_id=1, source_target_pairs={{0,8},{2,10},{4,12},{6,14},{8,0},{10,2},{12,4},{14,6},{1,9},{3,11}... | collective-permute-start | bytes 196616 | tf_op jit(solution)/shard_map/ppermute | solution.py:31
  226.4 6.2 %collective-permute-start.21 = (bf16[4,8192]{1,0:T(4,128)(2,1)S(1)}, bf16[4,8192]{1,0:T(4,128)(2,1)S(1)}, u32[]{:S(2)}, u32[]{:S(2)}) collective-permute-start(bf16[4,8192]{1,0:T(4,128)(2,1)S(1)} %get-tuple-element.149.refs_0_), channel_id=1, source_target_pairs={{0,12},{2,14},{4,8},{6,10},{8,4},{10,6},{12,0},{14,2},{1,13},{3,15... | collective-permute-start | bytes 196616 | tf_op jit(solution)/shard_map/ppermute | solution.py:31
  228.9 5.2 %collective-permute-start.20 = (bf16[4,8192]{1,0:T(4,128)(2,1)S(1)}, bf16[4,8192]{1,0:T(4,128)(2,1)S(1)}, u32[]{:S(2)}, u32[]{:S(2)}) collective-permute-start(bf16[4,8192]{1,0:T(4,128)(2,1)S(1)} %get-tuple-element.149.refs_0_), channel_id=1, source_target_pairs={{0,2},{2,0},{4,6},{6,4},{8,10},{10,8},{12,14},{14,12},{1,3},{3,1},... | collective-permute-start | bytes 196616 | tf_op jit(solution)/shard_map/ppermute | solution.py:61
  230.3 4.3 %collective-permute-start.26 = (bf16[4,8192]{1,0:T(4,128)(2,1)S(1)}, bf16[4,8192]{1,0:T(4,128)(2,1)S(1)}, u32[]{:S(2)}, u32[]{:S(2)}) collective-permute-start(bf16[4,8192]{1,0:T(4,128)(2,1)S(1)} %collective-permute-done.23.refs_4_), channel_id=1, source_target_pairs={{0,2},{2,0},{4,6},{6,4},{8,10},{10,8},{12,14},{14,12},{1,3},{3,1},... | collective-permute-start | bytes 196616 | tf_op jit(solution)/shard_map/ppermute | solution.py:61
  231.6 4.3 %collective-permute-start.25 = (bf16[4,8192]{1,0:T(4,128)(2,1)S(1)}, bf16[4,8192]{1,0:T(4,128)(2,1)S(1)}, u32[]{:S(2)}, u32[]{:S(2)}) collective-permute-start(bf16[4,8192]{1,0:T(4,128)(2,1)S(1)} %collective-permute-done.22.refs_3_), channel_id=1, source_target_pairs={{0,2},{2,0},{4,6},{6,4},{8,10},{10,8},{12,14},{14,12},{1,3},{3,1},... | collective-permute-start | bytes 196616 | tf_op jit(solution)/shard_map/ppermute | solution.py:61
  232.5 4.3 %collective-permute-start.24 = (bf16[4,8192]{1,0:T(4,128)(2,1)S(1)}, bf16[4,8192]{1,0:T(4,128)(2,1)S(1)}, u32[]{:S(2)}, u32[]{:S(2)}) collective-permute-start(bf16[4,8192]{1,0:T(4,128)(2,1)S(1)} %collective-permute-done.21.refs_2_), channel_id=1, source_target_pairs={{0,2},{2,0},{4,6},{6,4},{8,10},{10,8},{12,14},{14,12},{1,3},{3,1},... | collective-permute-start | bytes 196616 | tf_op jit(solution)/shard_map/ppermute | solution.py:61
  260.0 6.0 %collective-permute-start.30 = (bf16[4,8192]{1,0:T(4,128)(2,1)S(1)}, bf16[4,8192]{1,0:T(4,128)(2,1)S(1)}, u32[]{:S(2)}, u32[]{:S(2)}) collective-permute-start(bf16[4,8192]{1,0:T(4,128)(2,1)S(1)} %get-tuple-element.153.refs_0_), channel_id=1, source_target_pairs={{0,4},{2,6},{4,0},{6,2},{8,12},{10,14},{12,8},{14,10},{1,5},{3,7},... | collective-permute-start | bytes 196616 | tf_op jit(solution)/shard_map/ppermute | solution.py:31
  260.5 6.0 %collective-permute-start.29 = (bf16[4,8192]{1,0:T(4,128)(2,1)S(1)}, bf16[4,8192]{1,0:T(4,128)(2,1)S(1)}, u32[]{:S(2)}, u32[]{:S(2)}) collective-permute-start(bf16[4,8192]{1,0:T(4,128)(2,1)S(1)} %get-tuple-element.153.refs_0_), channel_id=1, source_target_pairs={{0,8},{2,10},{4,12},{6,14},{8,0},{10,2},{12,4},{14,6},{1,9},{3,11}... | collective-permute-start | bytes 196616 | tf_op jit(solution)/shard_map/ppermute | solution.py:31
  262.8 6.1 %collective-permute-start.28 = (bf16[4,8192]{1,0:T(4,128)(2,1)S(1)}, bf16[4,8192]{1,0:T(4,128)(2,1)S(1)}, u32[]{:S(2)}, u32[]{:S(2)}) collective-permute-start(bf16[4,8192]{1,0:T(4,128)(2,1)S(1)} %get-tuple-element.153.refs_0_), channel_id=1, source_target_pairs={{0,12},{2,14},{4,8},{6,10},{8,4},{10,6},{12,0},{14,2},{1,13},{3,15... | collective-permute-start | bytes 196616 | tf_op jit(solution)/shard_map/ppermute | solution.py:31
  264.5 6.2 %collective-permute-start.27 = (bf16[4,8192]{1,0:T(4,128)(2,1)S(1)}, bf16[4,8192]{1,0:T(4,128)(2,1)S(1)}, u32[]{:S(2)}, u32[]{:S(2)}) collective-permute-start(bf16[4,8192]{1,0:T(4,128)(2,1)S(1)} %get-tuple-element.153.refs_0_), channel_id=1, source_target_pairs={{0,2},{2,0},{4,6},{6,4},{8,10},{10,8},{12,14},{14,12},{1,3},{3,1},... | collective-permute-start | bytes 196616 | tf_op jit(solution)/shard_map/ppermute | solution.py:61
  266.1 4.6 %collective-permute-start.33 = (bf16[4,8192]{1,0:T(4,128)(2,1)S(1)}, bf16[4,8192]{1,0:T(4,128)(2,1)S(1)}, u32[]{:S(2)}, u32[]{:S(2)}) collective-permute-start(bf16[4,8192]{1,0:T(4,128)(2,1)S(1)} %collective-permute-done.30.refs_4_), channel_id=1, source_target_pairs={{0,2},{2,0},{4,6},{6,4},{8,10},{10,8},{12,14},{14,12},{1,3},{3,1},... | collective-permute-start | bytes 196616 | tf_op jit(solution)/shard_map/ppermute | solution.py:61
  266.5 4.5 %collective-permute-start.32 = (bf16[4,8192]{1,0:T(4,128)(2,1)S(1)}, bf16[4,8192]{1,0:T(4,128)(2,1)S(1)}, u32[]{:S(2)}, u32[]{:S(2)}) collective-permute-start(bf16[4,8192]{1,0:T(4,128)(2,1)S(1)} %collective-permute-done.29.refs_3_), channel_id=1, source_target_pairs={{0,2},{2,0},{4,6},{6,4},{8,10},{10,8},{12,14},{14,12},{1,3},{3,1},... | collective-permute-start | bytes 196616 | tf_op jit(solution)/shard_map/ppermute | solution.py:61
  268.9 4.3 %collective-permute-start.31 = (bf16[4,8192]{1,0:T(4,128)(2,1)S(1)}, bf16[4,8192]{1,0:T(4,128)(2,1)S(1)}, u32[]{:S(2)}, u32[]{:S(2)}) collective-permute-start(bf16[4,8192]{1,0:T(4,128)(2,1)S(1)} %collective-permute-done.28.refs_2_), channel_id=1, source_target_pairs={{0,2},{2,0},{4,6},{6,4},{8,10},{10,8},{12,14},{14,12},{1,3},{3,1},... | collective-permute-start | bytes 196616 | tf_op jit(solution)/shard_map/ppermute | solution.py:61
  273.1 21.2 %copy-start.1 = (s32[2,4,8]{2,1,0:T(4,128)S(1)}, s32[2,4,8]{2,1,0:T(4,128)}, u32[]{:S(2)}) copy-start(s32[2,4,8]{2,1,0:T(4,128)} %param.47) | copy-start | bytes 772
  (5 other events, 4.3 us)
where the time goes:
time: 297 us; the launch traced here: 295 us
  blocking collectives  119 us (40%)
  waiting for transfers between devices  51.5 us (17%)
  starting transfers between devices  50.2 us (17%)
  Pallas kernels  48.1 us (16%)
  local copies, waits for them, and re-layouts  12 us (4%)
  other arithmetic  11 us (4%)
  between operations  3.41 us (1%)
    all_to_all x4, blocking collectives, on_device(): lax.all_to_all(parts, 'tensor', split_axis=0, concat_axis=0, tiled=True)  65 us
    all_to_all x1, blocking collectives, exchange(): lax.all_to_all(pages.reshape(count, -1, 2 * HD), 'tensor', split_axis=0,...  53.6 us
    pallas_call x4, Pallas kernels, step(): pl.pallas_call(functools.partial(step_kernel, blocks, iteration, groups,...  31.2 us
    ppermute x4, waiting for transfers between devices, shift(): return lax.ppermute(rows, 'tensor', pairs)  28.2 us
    ppermute x15, waiting for transfers between devices, cross(): return lax.ppermute(value, 'tensor', [(r, r ^ 1) for r in range(8)])  20.2 us
    ppermute x15, starting transfers between devices, cross(): return lax.ppermute(value, 'tensor', [(r, r ^ 1) for r in range(8)])  18.8 us
    ppermute x9, starting transfers between devices, swap_xor(): return lax.ppermute(value, 'tensor', [(s, s ^ mask) for s in range(count)])  13.4 us
    ppermute x4, starting transfers between devices, shift(): return lax.ppermute(rows, 'tensor', pairs)  9.91 us
  transfers between devices with their start and end apart: 35, of which 18 were waited for; matrix products, arithmetic and copies ran while one was open for 6% of the time, Pallas kernels for 4%

commit v1 on v0

--- a/solution.py
+++ b/solution.py
@@ -17,7 +17,7 @@
 CHUNKS = 8
 PAGE = 16
 SURE = 16
-MORE = (0, 8, 12, 16, 18, 20, 22, 24, 26, 28, 30, 32, 34, 36, 40)
+MORE = (0, 12, 16, 20, 22, 24, 26, 28, 30, 32, 36, 40)
 VMEM_LIMIT = 10 * 1024 * 1024
 
 
@@ -199,11 +199,13 @@
 
 def project_kernel(rows, each, skipped, halves, *refs):
     heads = 2 if halves else 1
-    blocks, refs = refs[: -7 - halves - heads], refs[-7 - halves - heads :]
+    used = 7 + halves + 2 * heads
+    blocks, refs = refs[:-used], refs[-used:]
     starts_ref, begins_ref, cos_ref, sin_ref = refs[:4]
     weight_ref, part_refs = refs[4], refs[5 : 5 + halves]
     out_refs = refs[5 + halves : 5 + halves + heads]
-    states_ref, staged = refs[-2:]
+    states_ref, staged = refs[-2 - heads : -heads]
+    sum_refs = refs[-heads:]
     depth = weight_ref.shape[0] // CHUNKS
 
     def stage(span):
@@ -217,18 +219,20 @@
                 staged[here, :] = block[piece, :, span].astype(jnp.float32)
         return staged[...].astype(jnp.bfloat16)
 
-    totals = [jnp.zeros(out_ref.shape, jnp.float32) for out_ref in out_refs]
-    for c in range(CHUNKS):
-        span = slice(c * depth, (c + 1) * depth)
-        totals[0] += jnp.dot(stage(span), weight_ref[span, :], preferred_element_type=jnp.float32)
+    for sum_ref in sum_refs:
+        sum_ref[...] = jnp.zeros_like(sum_ref)
+
+    def add(sum_ref, weights, shift, count):
+        @pl.loop(0, count)
+        def _(c):
+            x = stage(pl.ds(pl.multiple_of(shift + c * depth, depth), depth))
+            here = pl.ds(pl.multiple_of(c * depth, depth), depth)
+            sum_ref[...] += jnp.dot(x, weights[here, :], preferred_element_type=jnp.float32)
+
+    add(sum_refs[0], weight_ref, 0, CHUNKS)
     for index, part_ref in enumerate(part_refs):
-        for c in range(part_ref.shape[0] // depth):
-            begin = pl.multiple_of(begins_ref[index] + c * depth, depth)
-            totals[1] += jnp.dot(
-                stage(pl.ds(begin, depth)),
-                part_ref[c * depth : (c + 1) * depth, :],
-                preferred_element_type=jnp.float32,
-            )
+        add(sum_refs[1], part_ref, begins_ref[index], part_ref.shape[0] // depth)
+    totals = [sum_ref[...] for sum_ref in sum_refs]
     for total, out_ref in zip(totals, out_refs):
         out_ref[:, HD:] = total[:, HD:].astype(jnp.bfloat16)
         for index in range(len(blocks)):
@@ -262,7 +266,10 @@
         out_shape=tuple(out_shape),
         in_specs=[whole()] * len(blocks) + [smem] * 2 + [whole()] * (3 + len(parts)),
         out_specs=tuple(whole() for _ in out_shape),
-        scratch_shapes=[pltpu.VMEM((len(blocks) * rows, width // CHUNKS), jnp.float32)],
+        scratch_shapes=[
+            pltpu.VMEM((len(blocks) * rows, width // CHUNKS), jnp.float32),
+            *[pltpu.VMEM(values.shape, jnp.float32)] * heads,
+        ],
         compiler_params=pltpu.CompilerParams(vmem_limit_bytes=2 * VMEM_LIMIT),
         cost_estimate=pl.CostEstimate(
             flops=2 * len(blocks) * rows * weight.size * heads,

time: 297 us -> 294 us (0.990); the launches traced: 295 us -> 295 us
  transfers between devices with their start and end apart: 35 -> 35, of which waited for: 18 -> 18; matrix products, arithmetic and copies ran while one was open for 6% -> 7% of each run, Pallas kernels for 4% -> 5%
where the time goes in v1:
time: 294 us; the launch traced here: 295 us
  blocking collectives  119 us (40%)
  waiting for transfers between devices  48.8 us (17%)
  Pallas kernels  48.7 us (17%)
  starting transfers between devices  48.6 us (17%)
  local copies, waits for them, and re-layouts  14 us (5%)
  other arithmetic  13.7 us (5%)
    all_to_all x4, blocking collectives, on_device(): lax.all_to_all(parts, 'tensor', split_axis=0, concat_axis=0, tiled=True)  65.1 us
    all_to_all x1, blocking collectives, exchange(): lax.all_to_all(pages.reshape(count, -1, 2 * HD), 'tensor', split_axis=0,...  53.6 us
    pallas_call x4, Pallas kernels, step(): pl.pallas_call(functools.partial(step_kernel, blocks, iteration, groups,...  31 us
    ppermute x4, waiting for transfers between devices, shift(): return lax.ppermute(rows, 'tensor', pairs)  25.6 us
    ppermute x15, waiting for transfers between devices, cross(): return lax.ppermute(value, 'tensor', [(r, r ^ 1) for r in range(8)])  20 us
    ppermute x15, starting transfers between devices, cross(): return lax.ppermute(value, 'tensor', [(r, r ^ 1) for r in range(8)])  18.2 us
    ppermute x9, starting transfers between devices, swap_xor(): return lax.ppermute(value, 'tensor', [(s, s ^ mask) for s in range(count)])  13.4 us
    ppermute x4, starting transfers between devices, shift(): return lax.ppermute(rows, 'tensor', pairs)  8.93 us
  transfers between devices with their start and end apart: 35, of which 18 were waited for; matrix products, arithmetic and copies ran while one was open for 7% of the time, Pallas kernels for 5%

profile of v1, /device:TPU:0, one launch (start us, length us, event | category | flops | bytes accessed | tf_op | source)
XLA Modules:
  0.0 295.4 jit_solution(11438311334355202534)
XLA Ops:
  0.7 2.3 prepare.1
  3.0 1.3 collective-permute-start.1
  4.3 5.6 %collective-permute-start = (bf16[17,4,8192]{2,1,0:T(4,128)(2,1)S(1)}, bf16[17,4,8192]{2,1,0:T(4,128)(2,1)S(1)}, u32[]{:S(2)}, u32[]{:S(2)}) collective-permute-start(bf16[17,4,8192]{2,1,0:T(4,128)(2,1)S(1)} %get-tuple-element.109.refs_0_), channel_id=1, source_target_pairs={{0,4},{2,6},{4,8},{6,10},{8,12},{10,14},{1,5},{3,7},{5,9},{7,11},{... | collective-permute-start | bytes 3342344 | tf_op jit(solution)/shard_map/ppermute | solution.py:77
  17.3 5.6 %parcels.1 = (bf16[8,17,16,256]{3,2,1,0:T(8,128)(2,1)}, bf16[8,48,16,256]{3,2,1,0:T(8,128)(2,1)}) custom-call(s32[4,16]{1,0:T(4,128)S(1)} %bitcast.44, s32[4]{0:T(128)S(1)} %dynamic_slice.17.used_ref, bf16[16,256]{1,0:T(8,128)(2,1)S(1)} %scatter.4.info_ref, bf16[64,16,2048]{2,1,0:T(8,128)(2,1)} %bitcast.57), custom_call_target="tpu_custom_call" | custom-call | tf_op jit(solution)/shard_map/parcels/pallas_call | solution.py:328
  24.0 8.5 %collective-permute-done.1 = bf16[17,4,8192]{2,1,0:T(4,128)(2,1)S(1)} collective-permute-done((bf16[17,4,8192]{2,1,0:T(4,128)(2,1)S(1)}, bf16[17,4,8192]{2,1,0:T(4,128)(2,1)S(1)}, u32[]{:S(2)}, u32[]{:S(2)}) %collective-permute-start.1) | collective-permute-done | bytes 1114144 | tf_op jit(solution)/shard_map/ppermute | solution.py:77
  32.5 1.2 collective-permute-done
  35.4 1.3 collective-permute-start.3
  40.0 3.0 %collective-permute-start.5 = (s32[1,1]{1,0:T(1,128)}, s32[1,1]{1,0:T(1,128)}, u32[]{:S(2)}, u32[]{:S(2)}) collective-permute-start(s32[1,1]{1,0:T(1,128)} %max.6), channel_id=1, source_target_pairs={{0,16},{16,0},{1,17},{17,1},{2,18},{18,2},{3,19},{19,3},{4,20},{20... | collective-permute-start | bytes 20 | tf_op jit(solution)/shard_map/ppermute | solution.py:678
  44.2 1.3 fusion.8
  45.5 3.1 %constant_dynamic-slice_fusion.1 = bf16[4096,256]{1,0:T(8,128)(2,1)} fusion(bf16[8192,256]{1,0:T(8,128)(2,1)} %refs_15_.1, s32[]{:T(128)S(6)} %select_n.121), kind=kLoop, calls=%fused_computation.39 | loop fusion | bytes 4194308 | tf_op jit(solution)/shard_map/dynamic_slice | solution.py:87
  48.6 1.7 collective-permute-start.7
  50.3 15.9 %collective-permute-done.3 = bf16[17,4,8192]{2,1,0:T(4,128)(2,1)} collective-permute-done((bf16[17,4,8192]{2,1,0:T(4,128)(2,1)}, bf16[17,4,8192]{2,1,0:T(4,128)(2,1)}, u32[]{:S(2)}, u32[]{:S(2)}) %collective-permute-start.3) | collective-permute-done | bytes 1114144 | tf_op jit(solution)/shard_map/ppermute | solution.py:77
  66.2 1.6 broadcast_select_fusion
  67.8 1.3 collective-permute-start.6
  69.7 57.0 %conditional.1 = (bf16[8,768,256]{2,1,0:T(8,128)(2,1)}) conditional(s32[]{:T(128)} %clamp.3, () %tuple.55, bf16[8,48,16,256]{3,2,1,0:T(8,128)(2,1)} %get-tuple-element.108, bf16[8,48,16,256]{3,2,1,0:T(8,128)(2,1)} %get-tuple-element.108, bf16[8,48,16,256]{3,2,1,0:T(8,128)(2,1)} %get-tuple-element.108, ...), branch_computations={%region_3.4_spmd, %region_4.5_spmd, %region_5.6_spmd, %region_6.7_... | conditional | bytes 18874402 | solution.py:731
  69.8 1.5 slice-done.6
  71.3 53.6 %all_to_all.79 = bf16[8,448,256]{2,1,0:T(8,128)(2,1)S(1)} all-to-all(bf16[8,448,256]{2,1,0:T(8,128)(2,1)S(1)} %bitcast.52), channel_id=1, replica_groups=mesh['groups'=2,'tensor'=8,'section'=2] {'tensor'}, dimensions={0} | all-to-all | bytes 3670016 | tf_op jit(solution)/shard_map/cond/branch_7_fun/all_to_all | solution.py:716
  124.8 1.9 pad.44
  126.8 3.7 %all-to-all-start.12 = ((bf16[8,272,256]{2,1,0:T(8,128)(2,1)}), bf16[8,272,256]{2,1,0:T(8,128)(2,1)S(1)}, u32[]{:S(2)}, u32[]{:S(2)}) async-start(bf16[8,272,256]{2,1,0:T(8,128)(2,1)} %bitcast.58), calls=%async_computation.12 | async-start | bytes 2228224 | tf_op jit(solution)/shard_map/all_to_all | solution.py:716
  130.6 3.9 %select_select_fusion.1 = (bf16[17,4,8192]{2,1,0:T(4,128)(2,1)S(1)}, bf16[17,4,8192]{2,1,0:T(4,128)(2,1)S(1)}, bf16[17,4,8192]{2,1,0:T(4,128)(2,1)S(1)}) fusion(bf16[17,4,8192]{2,1,0:T(4,128)(2,1)} %collective-permute-done.6, bf16[17,4,8192]{2,1,0:T(4,128)(2,1)} %collective-permute-done.3, bf16[17,4,8192]{2,1,0:T(4,128)(2,1)} %copy-done.13, pred[]{:T(512)S(6)} %eq.57, ...), kind=kLoop, calls=%fused_computation.3 | loop fusion | flops 5013504 | bytes 8912899 | tf_op jit(solution)/shard_map/jit(_where)/select_n | solution.py:80
  134.8 8.2 %project.1 = (bf16[256,256]{1,0:T(8,128)(2,1)}, bf16[256,256]{1,0:T(8,128)(2,1)S(1)}, bf16[4,4,8192]{2,1,0:T(4,128)(2,1)S(1)}) custom-call(bf16[17,4,8192]{2,1,0:T(4,128)(2,1)S(1)} %copy-done.4, bf16[17,4,8192]{2,1,0:T(4,128)(2,1)S(1)} %get-tuple-element.157.refs_1_, bf16[17,4,8192]{2,1,0:T(4,128)(2,1)S(1)} %get-tuple-element.156.refs_2_, ...), custom_call_target="tpu_custom_call" | custom-call | flops 2147483648 | bytes 8388608 | tf_op jit(solution)/shard_map/project/pallas_call | solution.py:264
  143.0 1.7 collective-permute-start.11
  146.0 6.3 %collective-permute-done.11 = bf16[256,256]{1,0:T(8,128)(2,1)S(1)} collective-permute-done((bf16[256,256]{1,0:T(8,128)(2,1)S(1)}, bf16[256,256]{1,0:T(8,128)(2,1)S(1)}, u32[]{:S(2)}, u32[]{:S(2)}) %collective-permute-start.11) | collective-permute-done | bytes 131104 | tf_op jit(solution)/shard_map/ppermute | solution.py:61
  152.4 5.5 %collective-permute-done.9.refs_1_ = bf16[4,4,8192]{2,1,0:T(4,128)(2,1)S(1)} collective-permute-done((bf16[4,4,8192]{2,1,0:T(4,128)(2,1)S(1)}, bf16[4,4,8192]{2,1,0:T(4,128)(2,1)S(1)}, u32[]{:S(2)}, u32[]{:S(2)}) %collective-permute-start.9) | collective-permute-done | bytes 262176 | tf_op jit(solution)/shard_map/ppermute | solution.py:61
  159.4 12.4 %decode_step.4 = (bf16[8,4,8192]{2,1,0:T(4,128)(2,1)S(1)}, bf16[32,256]{1,0:T(8,128)(2,1)S(1)}, bf16[8192,512]{1,0:T(8,128)(2,1)S(1)}, bf16[8192,256]{1,0:T(8,12...) custom-call(bf16[4,4,8192]{2,1,0:T(4,128)(2,1)S(1)} %copy-done.6, ...), custom_call_target="tpu_custom_call" | custom-call | flops 671088640 | bytes 25231360 | tf_op jit(solution)/shard_map/decode_step/pallas_call | solution.py:570
  171.8 18.8 %all_to_all.85.parts_ref = bf16[8,4,8192]{2,1,0:T(4,128)(2,1)S(1)} all-to-all(bf16[8,4,8192]{2,1,0:T(4,128)(2,1)S(1)} %get-tuple-element.131), channel_id=1, replica_groups=mesh['groups'=2,'tensor'=8,'section'=2] {'tensor'}, dimensions={0} | all-to-all | bytes 1048576 | tf_op jit(solution)/shard_map/all_to_all | solution.py:770
  192.8 2.6 collective-permute-start.14
  195.4 1.5 collective-permute-start.13
  197.4 1.5 collective-permute-done.15.refs_3_
  198.9 2.0 collective-permute-start.17
  201.1 2.1 collective-permute-done.18.refs_6_
  203.9 6.2 %decode_step.5 = (bf16[8,4,8192]{2,1,0:T(4,128)(2,1)S(1)}, bf16[32,256]{1,0:T(8,128)(2,1)S(1)}) custom-call(bf16[4,8192]{1,0:T(4,128)(2,1)S(1)} %get-tuple-element.134.refs_0_, bf16[4,8192]{1,0:T(4,128)(2,1)S(1)} %collective-permute-done.13.refs_1_, bf16[4,8192]{1,0:T(4,128)(2,1)S(1)} %collective-permute-done.14.refs_2_, ...), custom_call_target="tpu_custom_call" | custom-call | flops 671088640 | bytes 25231360 | tf_op jit(solution)/shard_map/decode_step/pallas_call | solution.py:570
  210.1 15.0 %all_to_all.86.parts_ref = bf16[8,4,8192]{2,1,0:T(4,128)(2,1)S(1)} all-to-all(bf16[8,4,8192]{2,1,0:T(4,128)(2,1)S(1)} %get-tuple-element.141), channel_id=1, replica_groups=mesh['groups'=2,'tensor'=8,'section'=2] {'tensor'}, dimensions={0} | all-to-all | bytes 1048576 | tf_op jit(solution)/shard_map/all_to_all | solution.py:770
  227.3 2.5 collective-permute-start.21
  229.9 1.5 collective-permute-start.20
  231.3 1.3 collective-permute-start.26
  233.5 1.5 collective-permute-start.24
  235.6 1.3 collective-permute-done.25.refs_6_
  237.8 6.2 %decode_step.6 = (bf16[8,4,8192]{2,1,0:T(4,128)(2,1)S(1)}, bf16[32,256]{1,0:T(8,128)(2,1)S(1)}) custom-call(bf16[4,8192]{1,0:T(4,128)(2,1)S(1)} %get-tuple-element.143.refs_0_, bf16[4,8192]{1,0:T(4,128)(2,1)S(1)} %collective-permute-done.20.refs_1_, bf16[4,8192]{1,0:T(4,128)(2,1)S(1)} %collective-permute-done.21.refs_2_, ...), custom_call_target="tpu_custom_call" | custom-call | flops 671088640 | bytes 25231360 | tf_op jit(solution)/shard_map/decode_step/pallas_call | solution.py:570
  244.0 16.8 %all_to_all.87.parts_ref = bf16[8,4,8192]{2,1,0:T(4,128)(2,1)S(1)} all-to-all(bf16[8,4,8192]{2,1,0:T(4,128)(2,1)S(1)} %get-tuple-element.145), channel_id=1, replica_groups=mesh['groups'=2,'tensor'=8,'section'=2] {'tensor'}, dimensions={0} | all-to-all | bytes 1048576 | tf_op jit(solution)/shard_map/all_to_all | solution.py:770
  261.3 2.2 collective-permute-start.29
  263.5 2.1 collective-permute-start.28
  265.6 1.6 collective-permute-start.27
  267.6 1.6 collective-permute-start.32
  269.6 1.8 collective-permute-start.31
  272.1 1.7 collective-permute-done.31.refs_5_
  273.8 6.2 %decode_step.7 = (bf16[8,4,8192]{2,1,0:T(4,128)(2,1)S(1)}, bf16[32,256]{1,0:T(8,128)(2,1)}) custom-call(bf16[4,8192]{1,0:T(4,128)(2,1)S(1)} %get-tuple-element.147.refs_0_, bf16[4,8192]{1,0:T(4,128)(2,1)S(1)} %collective-permute-done.27.refs_1_, bf16[4,8192]{1,0:T(4,128)(2,1)S(1)} %collective-permute-done.28.refs_2_, ...), custom_call_target="tpu_custom_call" | custom-call | flops 671088640 | bytes 25231360 | tf_op jit(solution)/shard_map/decode_step/pallas_call | solution.py:570
  280.1 14.5 %all_to_all.88.parts_ref = bf16[8,4,8192]{2,1,0:T(4,128)(2,1)S(1)} all-to-all(bf16[8,4,8192]{2,1,0:T(4,128)(2,1)S(1)} %get-tuple-element.149), channel_id=1, replica_groups=mesh['groups'=2,'tensor'=8,'section'=2] {'tensor'}, dimensions={0} | all-to-all | bytes 1048576 | tf_op jit(solution)/shard_map/all_to_all | solution.py:770
  (119 shorter events, 27.7 us)
Async XLA Ops:
  0.0 69.1 %copy-start = (s32[2,4,8]{2,1,0:T(4,128)S(1)}, s32[2,4,8]{2,1,0:T(4,128)}, u32[]{:S(2)}) copy-start(s32[2,4,8]{2,1,0:T(4,128)} %param.44) | copy-start | bytes 772
  3.0 19.9 %copy-start.3 = (bf16[17,4,8192]{2,1,0:T(4,128)(2,1)}, bf16[17,4,8192]{2,1,0:T(4,128)(2,1)S(1)}, u32[]{:S(2)}) copy-start(bf16[17,4,8192]{2,1,0:T(4,128)(2,1)S(1)} %get-tuple-element.109.refs_0_) | copy-start | bytes 3342340
  3.0 29.5 %collective-permute-start.1 = (bf16[17,4,8192]{2,1,0:T(4,128)(2,1)S(1)}, bf16[17,4,8192]{2,1,0:T(4,128)(2,1)S(1)}, u32[]{:S(2)}, u32[]{:S(2)}) collective-permute-start(bf16[17,4,8192]{2,1,0:T(4,128)(2,1)S(1)} %get-tuple-element.109.refs_0_), channel_id=1, source_target_pairs={{4,0},{6,2},{8,4},{10,6},{12,8},{14,10},{5,1},{7,3},{9,5},{11,7},{... | collective-permute-start | bytes 3342344 | tf_op jit(solution)/shard_map/ppermute | solution.py:77
  4.3 29.4 %collective-permute-start = (bf16[17,4,8192]{2,1,0:T(4,128)(2,1)S(1)}, bf16[17,4,8192]{2,1,0:T(4,128)(2,1)S(1)}, u32[]{:S(2)}, u32[]{:S(2)}) collective-permute-start(bf16[17,4,8192]{2,1,0:T(4,128)(2,1)S(1)} %get-tuple-element.109.refs_0_), channel_id=1, source_target_pairs={{0,4},{2,6},{4,8},{6,10},{8,12},{10,14},{1,5},{3,7},{5,9},{7,11},{... | collective-permute-start | bytes 3342344 | tf_op jit(solution)/shard_map/ppermute | solution.py:77
  11.5 27.3 %collective-permute-start.4 = (s32[1,1]{1,0:T(1,128)}, s32[1,1]{1,0:T(1,128)}, u32[]{:S(2)}, u32[]{:S(2)}) collective-permute-start(s32[1,1]{1,0:T(1,128)} %bitcast.18), channel_id=1, source_target_pairs={{0,1},{1,0},{2,3},{3,2},{4,5},{5,4},{6,7},{7,6},{8,9},{9,8},{10,11... | collective-permute-start | bytes 20 | tf_op jit(solution)/shard_map/ppermute | solution.py:678
  17.3 5.6 %copy-start.11 = (s32[1,32]{1,0:T(1,128)S(1)}, s32[1,32]{1,0:T(1,128)}, u32[]{:S(2)}) copy-start(s32[1,32]{1,0:T(1,128)} %param.42) | copy-start | bytes 388
  17.3 6.0 %copy-start.16 = (s32[32]{0:T(128)S(1)}, s32[32]{0:T(128)}, u32[]{:S(2)}) copy-start(s32[32]{0:T(128)} %reshape.179) | copy-start | bytes 388
  17.3 6.0 %copy-start.17 = (s32[32]{0:T(128)S(1)}, s32[32]{0:T(128)}, u32[]{:S(2)}) copy-start(s32[32]{0:T(128)} %reshape.180) | copy-start | bytes 388
  34.7 15.6 %collective-permute-start.2 = (bf16[17,4,8192]{2,1,0:T(4,128)(2,1)}, bf16[17,4,8192]{2,1,0:T(4,128)(2,1)S(1)}, u32[]{:S(2)}, u32[]{:S(2)}) collective-permute-start(bf16[17,4,8192]{2,1,0:T(4,128)(2,1)} %copy-done.15), channel_id=1, source_target_pairs={{4,8},{6,10},{8,12},{10,14},{5,9},{7,11},{9,13},{11,15},{20,24},{2... | collective-permute-start | bytes 3342344 | tf_op jit(solution)/shard_map/ppermute | solution.py:77
  35.4 30.8 %collective-permute-start.3 = (bf16[17,4,8192]{2,1,0:T(4,128)(2,1)}, bf16[17,4,8192]{2,1,0:T(4,128)(2,1)}, u32[]{:S(2)}, u32[]{:S(2)}) collective-permute-start(bf16[17,4,8192]{2,1,0:T(4,128)(2,1)} %copy-done.14), channel_id=1, source_target_pairs={{4,0},{6,2},{8,4},{10,6},{5,1},{7,3},{9,5},{11,7},{20,16},{22,18},... | collective-permute-start | bytes 3342344 | tf_op jit(solution)/shard_map/ppermute | solution.py:77
  40.0 3.6 %collective-permute-start.5 = (s32[1,1]{1,0:T(1,128)}, s32[1,1]{1,0:T(1,128)}, u32[]{:S(2)}, u32[]{:S(2)}) collective-permute-start(s32[1,1]{1,0:T(1,128)} %max.6), channel_id=1, source_target_pairs={{0,16},{16,0},{1,17},{17,1},{2,18},{18,2},{3,19},{19,3},{4,20},{20... | collective-permute-start | bytes 20 | tf_op jit(solution)/shard_map/ppermute | solution.py:678
  48.6 78.1 %collective-permute-start.7 = (bf16[4096,256]{1,0:T(8,128)(2,1)}, bf16[4096,256]{1,0:T(8,128)(2,1)S(1)}, u32[]{:S(2)}, u32[]{:S(2)}) collective-permute-start(bf16[4096,256]{1,0:T(8,128)(2,1)} %constant_dynamic-slice_fusion.1), channel_id=1, source_target_pairs={{0,2},{2,0},{4,6},{6,4},{8,10},{10,8},{12,14},{14,12},{1,3},{3,1},... | collective-permute-start | bytes 6291464 | tf_op jit(solution)/shard_map/ppermute | solution.py:61
  50.3 19.4 %copy-start.13 = (bf16[17,4,8192]{2,1,0:T(4,128)(2,1)}, bf16[17,4,8192]{2,1,0:T(4,128)(2,1)S(1)}, u32[]{:S(2)}) copy-start(bf16[17,4,8192]{2,1,0:T(4,128)(2,1)S(1)} %collective-permute-done.2) | copy-start | bytes 3342340
  67.8 59.0 %collective-permute-start.6 = (bf16[17,4,8192]{2,1,0:T(4,128)(2,1)}, bf16[17,4,8192]{2,1,0:T(4,128)(2,1)}, u32[]{:S(2)}, u32[]{:S(2)}) collective-permute-start(bf16[17,4,8192]{2,1,0:T(4,128)(2,1)} %broadcast_select_fusion), channel_id=1, source_target_pairs={{4,0},{6,2},{8,12},{10,14},{5,1},{7,3},{9,13},{11,15},{20,16},{22,... | collective-permute-start | bytes 3342344 | tf_op jit(solution)/shard_map/ppermute | solution.py:92
  126.7 7.8 %collective-permute-start.8 = (bf16[4096,256]{1,0:T(8,128)(2,1)S(1)}, bf16[4096,256]{1,0:T(8,128)(2,1)}, u32[]{:S(2)}, u32[]{:S(2)}) collective-permute-start(bf16[4096,256]{1,0:T(8,128)(2,1)S(1)} %collective-permute-done.7.refs_9_), channel_id=1, source_target_pairs={{0,1},{1,0},{2,3},{3,2},{4,5},{5,4},{6,7},{7,6},{8,9},{9,8},{10,11... | collective-permute-start | bytes 6291464 | tf_op jit(solution)/shard_map/ppermute | solution.py:96
  126.8 31.6 %all-to-all-start.12 = ((bf16[8,272,256]{2,1,0:T(8,128)(2,1)}), bf16[8,272,256]{2,1,0:T(8,128)(2,1)S(1)}, u32[]{:S(2)}, u32[]{:S(2)}) async-start(bf16[8,272,256]{2,1,0:T(8,128)(2,1)} %bitcast.58), calls=%async_computation.12 | async-start | bytes 2228224 | tf_op jit(solution)/shard_map/all_to_all | solution.py:716
  130.6 4.0 %copy-start.2 = (bf16[8192,256]{1,0:T(8,128)(2,1)S(1)}, bf16[8192,256]{1,0:T(8,128)(2,1)}, u32[]{:S(2)}) copy-start(bf16[8192,256]{1,0:T(8,128)(2,1)} %refs_15_.1) | copy-start | bytes 12582916
  130.6 4.2 %copy-start.4 = (bf16[17,4,8192]{2,1,0:T(4,128)(2,1)S(1)}, bf16[17,4,8192]{2,1,0:T(4,128)(2,1)}, u32[]{:S(2)}) copy-start(bf16[17,4,8192]{2,1,0:T(4,128)(2,1)} %copy-done.3) | copy-start | bytes 3342340
  130.6 4.2 %copy-start.7 = (f32[128,128]{1,0:T(8,128)S(1)}, f32[128,128]{1,0:T(8,128)}, u32[]{:S(2)}) copy-start(f32[128,128]{1,0:T(8,128)} %constant.216.clone.refs_7_) | copy-start | bytes 196612
  130.6 4.2 %copy-start.8 = (f32[128,128]{1,0:T(8,128)S(1)}, f32[128,128]{1,0:T(8,128)}, u32[]{:S(2)}) copy-start(f32[128,128]{1,0:T(8,128)} %constant.215.clone.refs_6_) | copy-start | bytes 196612
  134.8 11.1 %copy-start.18 = (s32[2,4]{1,0:T(2,128)S(1)}, s32[2,4]{1,0:T(2,128)}, u32[]{:S(2)}) copy-start(s32[2,4]{1,0:T(2,128)} %param.43) | copy-start | bytes 100
  134.8 11.1 %copy-start.10 = (bf16[8192]{0:T(1024)(128)(2,1)S(1)}, bf16[8192]{0:T(1024)(128)(2,1)}, u32[]{:S(2)}) copy-start(bf16[8192]{0:T(1024)(128)(2,1)} %param.36) | copy-start | bytes 49156
  143.0 9.4 %collective-permute-start.11 = (bf16[256,256]{1,0:T(8,128)(2,1)S(1)}, bf16[256,256]{1,0:T(8,128)(2,1)S(1)}, u32[]{:S(2)}, u32[]{:S(2)}) collective-permute-start(bf16[256,256]{1,0:T(8,128)(2,1)S(1)} %get-tuple-element.127), channel_id=1, source_target_pairs={{0,2},{2,0},{4,6},{6,4},{8,10},{10,8},{12,14},{14,12},{1,3},{3,1},... | collective-permute-start | bytes 393224 | tf_op jit(solution)/shard_map/ppermute | solution.py:61
  144.8 13.0 %collective-permute-start.9 = (bf16[4,4,8192]{2,1,0:T(4,128)(2,1)S(1)}, bf16[4,4,8192]{2,1,0:T(4,128)(2,1)S(1)}, u32[]{:S(2)}, u32[]{:S(2)}) collective-permute-start(bf16[4,4,8192]{2,1,0:T(4,128)(2,1)S(1)} %get-tuple-element.121.refs_0_), channel_id=1, source_target_pairs={{0,2},{2,0},{4,6},{6,4},{8,10},{10,8},{12,14},{14,12},{1,3},{3,1},... | collective-permute-start | bytes 786440 | tf_op jit(solution)/shard_map/ppermute | solution.py:61
  145.9 12.5 %collective-permute-start.10 = (bf16[256,256]{1,0:T(8,128)(2,1)}, bf16[256,256]{1,0:T(8,128)(2,1)S(1)}, u32[]{:S(2)}, u32[]{:S(2)}) collective-permute-start(bf16[256,256]{1,0:T(8,128)(2,1)} %get-tuple-element.126), channel_id=1, source_target_pairs={{0,1},{1,0},{2,3},{3,2},{4,5},{5,4},{6,7},{7,6},{8,9},{9,8},{10,11... | collective-permute-start | bytes 393224 | tf_op jit(solution)/shard_map/ppermute | solution.py:752
  152.3 6.1 %collective-permute-start.12 = (bf16[256,256]{1,0:T(8,128)(2,1)S(1)}, bf16[256,256]{1,0:T(8,128)(2,1)S(1)}, u32[]{:S(2)}, u32[]{:S(2)}) collective-permute-start(bf16[256,256]{1,0:T(8,128)(2,1)S(1)} %collective-permute-done.11), channel_id=1, source_target_pairs={{0,1},{1,0},{2,3},{3,2},{4,5},{5,4},{6,7},{7,6},{8,9},{9,8},{10,11... | collective-permute-start | bytes 393224 | tf_op jit(solution)/shard_map/ppermute | solution.py:752
  190.9 5.9 %collective-permute-start.16 = (bf16[4,8192]{1,0:T(4,128)(2,1)S(1)}, bf16[4,8192]{1,0:T(4,128)(2,1)S(1)}, u32[]{:S(2)}, u32[]{:S(2)}) collective-permute-start(bf16[4,8192]{1,0:T(4,128)(2,1)S(1)} %get-tuple-element.134.refs_0_), channel_id=1, source_target_pairs={{0,4},{2,6},{4,0},{6,2},{8,12},{10,14},{12,8},{14,10},{1,5},{3,7},... | collective-permute-start | bytes 196616 | tf_op jit(solution)/shard_map/ppermute | solution.py:31
  192.1 6.9 %collective-permute-start.15 = (bf16[4,8192]{1,0:T(4,128)(2,1)S(1)}, bf16[4,8192]{1,0:T(4,128)(2,1)S(1)}, u32[]{:S(2)}, u32[]{:S(2)}) collective-permute-start(bf16[4,8192]{1,0:T(4,128)(2,1)S(1)} %get-tuple-element.134.refs_0_), channel_id=1, source_target_pairs={{0,8},{2,10},{4,12},{6,14},{8,0},{10,2},{12,4},{14,6},{1,9},{3,11}... | collective-permute-start | bytes 196616 | tf_op jit(solution)/shard_map/ppermute | solution.py:31
  192.8 6.2 %collective-permute-start.14 = (bf16[4,8192]{1,0:T(4,128)(2,1)S(1)}, bf16[4,8192]{1,0:T(4,128)(2,1)S(1)}, u32[]{:S(2)}, u32[]{:S(2)}) collective-permute-start(bf16[4,8192]{1,0:T(4,128)(2,1)S(1)} %get-tuple-element.134.refs_0_), channel_id=1, source_target_pairs={{0,12},{2,14},{4,8},{6,10},{8,4},{10,6},{12,0},{14,2},{1,13},{3,15... | collective-permute-start | bytes 196616 | tf_op jit(solution)/shard_map/ppermute | solution.py:31
  195.4 5.6 %collective-permute-start.13 = (bf16[4,8192]{1,0:T(4,128)(2,1)S(1)}, bf16[4,8192]{1,0:T(4,128)(2,1)S(1)}, u32[]{:S(2)}, u32[]{:S(2)}) collective-permute-start(bf16[4,8192]{1,0:T(4,128)(2,1)S(1)} %get-tuple-element.134.refs_0_), channel_id=1, source_target_pairs={{0,2},{2,0},{4,6},{6,4},{8,10},{10,8},{12,14},{14,12},{1,3},{3,1},... | collective-permute-start | bytes 196616 | tf_op jit(solution)/shard_map/ppermute | solution.py:61
  196.8 4.3 %collective-permute-start.19 = (bf16[4,8192]{1,0:T(4,128)(2,1)S(1)}, bf16[4,8192]{1,0:T(4,128)(2,1)S(1)}, u32[]{:S(2)}, u32[]{:S(2)}) collective-permute-start(bf16[4,8192]{1,0:T(4,128)(2,1)S(1)} %collective-permute-done.16.refs_4_), channel_id=1, source_target_pairs={{0,2},{2,0},{4,6},{6,4},{8,10},{10,8},{12,14},{14,12},{1,3},{3,1},... | collective-permute-start | bytes 196616 | tf_op jit(solution)/shard_map/ppermute | solution.py:61
  198.9 4.3 %collective-permute-start.18 = (bf16[4,8192]{1,0:T(4,128)(2,1)S(1)}, bf16[4,8192]{1,0:T(4,128)(2,1)S(1)}, u32[]{:S(2)}, u32[]{:S(2)}) collective-permute-start(bf16[4,8192]{1,0:T(4,128)(2,1)S(1)} %collective-permute-done.15.refs_3_), channel_id=1, source_target_pairs={{0,2},{2,0},{4,6},{6,4},{8,10},{10,8},{12,14},{14,12},{1,3},{3,1},... | collective-permute-start | bytes 196616 | tf_op jit(solution)/shard_map/ppermute | solution.py:61
  198.9 5.0 %collective-permute-start.17 = (bf16[4,8192]{1,0:T(4,128)(2,1)S(1)}, bf16[4,8192]{1,0:T(4,128)(2,1)S(1)}, u32[]{:S(2)}, u32[]{:S(2)}) collective-permute-start(bf16[4,8192]{1,0:T(4,128)(2,1)S(1)} %collective-permute-done.14.refs_2_), channel_id=1, source_target_pairs={{0,2},{2,0},{4,6},{6,4},{8,10},{10,8},{12,14},{14,12},{1,3},{3,1},... | collective-permute-start | bytes 196616 | tf_op jit(solution)/shard_map/ppermute | solution.py:61
  225.4 5.9 %collective-permute-start.23 = (bf16[4,8192]{1,0:T(4,128)(2,1)S(1)}, bf16[4,8192]{1,0:T(4,128)(2,1)S(1)}, u32[]{:S(2)}, u32[]{:S(2)}) collective-permute-start(bf16[4,8192]{1,0:T(4,128)(2,1)S(1)} %get-tuple-element.143.refs_0_), channel_id=1, source_target_pairs={{0,4},{2,6},{4,0},{6,2},{8,12},{10,14},{12,8},{14,10},{1,5},{3,7},... | collective-permute-start | bytes 196616 | tf_op jit(solution)/shard_map/ppermute | solution.py:31
  226.6 6.0 %collective-permute-start.22 = (bf16[4,8192]{1,0:T(4,128)(2,1)S(1)}, bf16[4,8192]{1,0:T(4,128)(2,1)S(1)}, u32[]{:S(2)}, u32[]{:S(2)}) collective-permute-start(bf16[4,8192]{1,0:T(4,128)(2,1)S(1)} %get-tuple-element.143.refs_0_), channel_id=1, source_target_pairs={{0,8},{2,10},{4,12},{6,14},{8,0},{10,2},{12,4},{14,6},{1,9},{3,11}... | collective-permute-start | bytes 196616 | tf_op jit(solution)/shard_map/ppermute | solution.py:31
  227.3 6.2 %collective-permute-start.21 = (bf16[4,8192]{1,0:T(4,128)(2,1)S(1)}, bf16[4,8192]{1,0:T(4,128)(2,1)S(1)}, u32[]{:S(2)}, u32[]{:S(2)}) collective-permute-start(bf16[4,8192]{1,0:T(4,128)(2,1)S(1)} %get-tuple-element.143.refs_0_), channel_id=1, source_target_pairs={{0,12},{2,14},{4,8},{6,10},{8,4},{10,6},{12,0},{14,2},{1,13},{3,15... | collective-permute-start | bytes 196616 | tf_op jit(solution)/shard_map/ppermute | solution.py:31
  229.9 5.2 %collective-permute-start.20 = (bf16[4,8192]{1,0:T(4,128)(2,1)S(1)}, bf16[4,8192]{1,0:T(4,128)(2,1)S(1)}, u32[]{:S(2)}, u32[]{:S(2)}) collective-permute-start(bf16[4,8192]{1,0:T(4,128)(2,1)S(1)} %get-tuple-element.143.refs_0_), channel_id=1, source_target_pairs={{0,2},{2,0},{4,6},{6,4},{8,10},{10,8},{12,14},{14,12},{1,3},{3,1},... | collective-permute-start | bytes 196616 | tf_op jit(solution)/shard_map/ppermute | solution.py:61
  231.3 4.3 %collective-permute-start.26 = (bf16[4,8192]{1,0:T(4,128)(2,1)S(1)}, bf16[4,8192]{1,0:T(4,128)(2,1)S(1)}, u32[]{:S(2)}, u32[]{:S(2)}) collective-permute-start(bf16[4,8192]{1,0:T(4,128)(2,1)S(1)} %collective-permute-done.23.refs_4_), channel_id=1, source_target_pairs={{0,2},{2,0},{4,6},{6,4},{8,10},{10,8},{12,14},{14,12},{1,3},{3,1},... | collective-permute-start | bytes 196616 | tf_op jit(solution)/shard_map/ppermute | solution.py:61
  232.6 4.3 %collective-permute-start.25 = (bf16[4,8192]{1,0:T(4,128)(2,1)S(1)}, bf16[4,8192]{1,0:T(4,128)(2,1)S(1)}, u32[]{:S(2)}, u32[]{:S(2)}) collective-permute-start(bf16[4,8192]{1,0:T(4,128)(2,1)S(1)} %collective-permute-done.22.refs_3_), channel_id=1, source_target_pairs={{0,2},{2,0},{4,6},{6,4},{8,10},{10,8},{12,14},{14,12},{1,3},{3,1},... | collective-permute-start | bytes 196616 | tf_op jit(solution)/shard_map/ppermute | solution.py:61
  233.5 4.3 %collective-permute-start.24 = (bf16[4,8192]{1,0:T(4,128)(2,1)S(1)}, bf16[4,8192]{1,0:T(4,128)(2,1)S(1)}, u32[]{:S(2)}, u32[]{:S(2)}) collective-permute-start(bf16[4,8192]{1,0:T(4,128)(2,1)S(1)} %collective-permute-done.21.refs_2_), channel_id=1, source_target_pairs={{0,2},{2,0},{4,6},{6,4},{8,10},{10,8},{12,14},{14,12},{1,3},{3,1},... | collective-permute-start | bytes 196616 | tf_op jit(solution)/shard_map/ppermute | solution.py:61
  261.1 6.0 %collective-permute-start.30 = (bf16[4,8192]{1,0:T(4,128)(2,1)S(1)}, bf16[4,8192]{1,0:T(4,128)(2,1)S(1)}, u32[]{:S(2)}, u32[]{:S(2)}) collective-permute-start(bf16[4,8192]{1,0:T(4,128)(2,1)S(1)} %get-tuple-element.147.refs_0_), channel_id=1, source_target_pairs={{0,4},{2,6},{4,0},{6,2},{8,12},{10,14},{12,8},{14,10},{1,5},{3,7},... | collective-permute-start | bytes 196616 | tf_op jit(solution)/shard_map/ppermute | solution.py:31
  261.3 6.3 %collective-permute-start.29 = (bf16[4,8192]{1,0:T(4,128)(2,1)S(1)}, bf16[4,8192]{1,0:T(4,128)(2,1)S(1)}, u32[]{:S(2)}, u32[]{:S(2)}) collective-permute-start(bf16[4,8192]{1,0:T(4,128)(2,1)S(1)} %get-tuple-element.147.refs_0_), channel_id=1, source_target_pairs={{0,8},{2,10},{4,12},{6,14},{8,0},{10,2},{12,4},{14,6},{1,9},{3,11}... | collective-permute-start | bytes 196616 | tf_op jit(solution)/shard_map/ppermute | solution.py:31
  263.5 6.1 %collective-permute-start.28 = (bf16[4,8192]{1,0:T(4,128)(2,1)S(1)}, bf16[4,8192]{1,0:T(4,128)(2,1)S(1)}, u32[]{:S(2)}, u32[]{:S(2)}) collective-permute-start(bf16[4,8192]{1,0:T(4,128)(2,1)S(1)} %get-tuple-element.147.refs_0_), channel_id=1, source_target_pairs={{0,12},{2,14},{4,8},{6,10},{8,4},{10,6},{12,0},{14,2},{1,13},{3,15... | collective-permute-start | bytes 196616 | tf_op jit(solution)/shard_map/ppermute | solution.py:31
  265.6 5.8 %collective-permute-start.27 = (bf16[4,8192]{1,0:T(4,128)(2,1)S(1)}, bf16[4,8192]{1,0:T(4,128)(2,1)S(1)}, u32[]{:S(2)}, u32[]{:S(2)}) collective-permute-start(bf16[4,8192]{1,0:T(4,128)(2,1)S(1)} %get-tuple-element.147.refs_0_), channel_id=1, source_target_pairs={{0,2},{2,0},{4,6},{6,4},{8,10},{10,8},{12,14},{14,12},{1,3},{3,1},... | collective-permute-start | bytes 196616 | tf_op jit(solution)/shard_map/ppermute | solution.py:61
  267.1 4.3 %collective-permute-start.33 = (bf16[4,8192]{1,0:T(4,128)(2,1)S(1)}, bf16[4,8192]{1,0:T(4,128)(2,1)S(1)}, u32[]{:S(2)}, u32[]{:S(2)}) collective-permute-start(bf16[4,8192]{1,0:T(4,128)(2,1)S(1)} %collective-permute-done.30.refs_4_), channel_id=1, source_target_pairs={{0,2},{2,0},{4,6},{6,4},{8,10},{10,8},{12,14},{14,12},{1,3},{3,1},... | collective-permute-start | bytes 196616 | tf_op jit(solution)/shard_map/ppermute | solution.py:61
  267.6 4.5 %collective-permute-start.32 = (bf16[4,8192]{1,0:T(4,128)(2,1)S(1)}, bf16[4,8192]{1,0:T(4,128)(2,1)S(1)}, u32[]{:S(2)}, u32[]{:S(2)}) collective-permute-start(bf16[4,8192]{1,0:T(4,128)(2,1)S(1)} %collective-permute-done.29.refs_3_), channel_id=1, source_target_pairs={{0,2},{2,0},{4,6},{6,4},{8,10},{10,8},{12,14},{14,12},{1,3},{3,1},... | collective-permute-start | bytes 196616 | tf_op jit(solution)/shard_map/ppermute | solution.py:61
  269.6 4.3 %collective-permute-start.31 = (bf16[4,8192]{1,0:T(4,128)(2,1)S(1)}, bf16[4,8192]{1,0:T(4,128)(2,1)S(1)}, u32[]{:S(2)}, u32[]{:S(2)}) collective-permute-start(bf16[4,8192]{1,0:T(4,128)(2,1)S(1)} %collective-permute-done.28.refs_2_), channel_id=1, source_target_pairs={{0,2},{2,0},{4,6},{6,4},{8,10},{10,8},{12,14},{14,12},{1,3},{3,1},... | collective-permute-start | bytes 196616 | tf_op jit(solution)/shard_map/ppermute | solution.py:61
  273.8 21.5 %copy-start.1 = (s32[2,4,8]{2,1,0:T(4,128)S(1)}, s32[2,4,8]{2,1,0:T(4,128)}, u32[]{:S(2)}) copy-start(s32[2,4,8]{2,1,0:T(4,128)} %param.44) | copy-start | bytes 772
  (7 other events, 6.8 us)

commit v2 on v1

--- a/solution.py
+++ b/solution.py
@@ -16,8 +16,8 @@
 LANES = 8
 CHUNKS = 8
 PAGE = 16
-SURE = 16
-MORE = (0, 12, 16, 20, 22, 24, 26, 28, 30, 32, 36, 40)
+SURE = 14
+MORE = (0, 14, 18, 22, 24, 26, 28, 30, 32, 34, 38, 42)
 VMEM_LIMIT = 10 * 1024 * 1024
 
 
@@ -222,16 +222,24 @@
     for sum_ref in sum_refs:
         sum_ref[...] = jnp.zeros_like(sum_ref)
 
-    def add(sum_ref, weights, shift, count):
+    def add(shift, count, part_ref=None):
         @pl.loop(0, count)
         def _(c):
-            x = stage(pl.ds(pl.multiple_of(shift + c * depth, depth), depth))
-            here = pl.ds(pl.multiple_of(c * depth, depth), depth)
-            sum_ref[...] += jnp.dot(x, weights[here, :], preferred_element_type=jnp.float32)
-
-    add(sum_refs[0], weight_ref, 0, CHUNKS)
+            there = pl.ds(pl.multiple_of(shift + c * depth, depth), depth)
+            x = stage(there)
+            sum_refs[0][...] += jnp.dot(
+                x, weight_ref[there, :], preferred_element_type=jnp.float32
+            )
+            if part_ref is not None:
+                here = pl.ds(pl.multiple_of(c * depth, depth), depth)
+                sum_refs[1][...] += jnp.dot(
+                    x, part_ref[here, :], preferred_element_type=jnp.float32
+                )
+
+    if not halves:
+        add(0, CHUNKS)
     for index, part_ref in enumerate(part_refs):
-        add(sum_refs[1], part_ref, begins_ref[index], part_ref.shape[0] // depth)
+        add(begins_ref[index], part_ref.shape[0] // depth, part_ref)
     totals = [sum_ref[...] for sum_ref in sum_refs]
     for total, out_ref in zip(totals, out_refs):
         out_ref[:, HD:] = total[:, HD:].astype(jnp.bfloat16)
@@ -270,7 +278,7 @@
             pltpu.VMEM((len(blocks) * rows, width // CHUNKS), jnp.float32),
             *[pltpu.VMEM(values.shape, jnp.float32)] * heads,
         ],
-        compiler_params=pltpu.CompilerParams(vmem_limit_bytes=2 * VMEM_LIMIT),
+        compiler_params=pltpu.CompilerParams(vmem_limit_bytes=VMEM_LIMIT),
         cost_estimate=pl.CostEstimate(
             flops=2 * len(blocks) * rows * weight.size * heads,
             bytes_accessed=2 * weight.size * heads,

time: 294 us -> 292 us (level)
  blocking collectives: 119 us -> 116 us
  transfers between devices with their start and end apart: 35 -> 35, of which waited for: 18 -> 17; matrix products, arithmetic and copies ran while one was open for 7% -> 8% of each run, Pallas kernels for 5% -> 4%
where the time goes in v2:
time: 292 us
  blocking collectives  116 us (40%)
  starting transfers between devices  49.2 us (17%)
  waiting for transfers between devices  47.2 us (16%)
  Pallas kernels  46.9 us (16%)
  local copies, waits for them, and re-layouts  15.3 us (5%)
  other arithmetic  14.1 us (5%)
  between operations  3.15 us (1%)
    all_to_all x4, blocking collectives, on_device(): lax.all_to_all(parts, 'tensor', split_axis=0, concat_axis=0, tiled=True)  65.4 us
    all_to_all x1, blocking collectives, exchange(): lax.all_to_all(pages.reshape(count, -1, 2 * HD), 'tensor', split_axis=0,...  50.8 us
    pallas_call x4, Pallas kernels, step(): pl.pallas_call(functools.partial(step_kernel, blocks, iteration, groups,...  31.1 us
    ppermute x4, waiting for transfers between devices, shift(): return lax.ppermute(rows, 'tensor', pairs)  25 us
    ppermute x15, waiting for transfers between devices, cross(): return lax.ppermute(value, 'tensor', [(r, r ^ 1) for r in range(8)])  20.2 us
    ppermute x15, starting transfers between devices, cross(): return lax.ppermute(value, 'tensor', [(r, r ^ 1) for r in range(8)])  18.8 us
    ppermute x9, starting transfers between devices, swap_xor(): return lax.ppermute(value, 'tensor', [(s, s ^ mask) for s in range(count)])  13.4 us
    ppermute x4, starting transfers between devices, shift(): return lax.ppermute(rows, 'tensor', pairs)  8.93 us
  transfers between devices with their start and end apart: 35, of which 17 were waited for; matrix products, arithmetic and copies ran while one was open for 8% of the time, Pallas kernels for 4%

profile of v2, /device:TPU:0, one launch (start us, length us, event | category | flops | bytes accessed | tf_op | source)
XLA Modules:
  0.0 292.1 jit_solution(3258937648104283392)
XLA Ops:
  0.7 2.3 prepare.1
  3.0 1.3 collective-permute-start.1
  4.3 5.6 %collective-permute-start = (bf16[17,4,8192]{2,1,0:T(4,128)(2,1)S(1)}, bf16[17,4,8192]{2,1,0:T(4,128)(2,1)S(1)}, u32[]{:S(2)}, u32[]{:S(2)}) collective-permute-start(bf16[17,4,8192]{2,1,0:T(4,128)(2,1)S(1)} %get-tuple-element.109.refs_0_), channel_id=1, source_target_pairs={{0,4},{2,6},{4,8},{6,10},{8,12},{10,14},{1,5},{3,7},{5,9},{7,11},{... | collective-permute-start | bytes 3342344 | tf_op jit(solution)/shard_map/ppermute | solution.py:77
  13.1 1.3 fusion.11
  18.5 5.6 %parcels.1 = (bf16[8,15,16,256]{3,2,1,0:T(8,128)(2,1)}, bf16[8,50,16,256]{3,2,1,0:T(8,128)(2,1)}) custom-call(s32[4,16]{1,0:T(4,128)S(1)} %bitcast.44, s32[4]{0:T(128)S(1)} %dynamic_slice.17.used_ref, bf16[16,256]{1,0:T(8,128)(2,1)S(1)} %scatter.4.info_ref, bf16[64,16,2048]{2,1,0:T(8,128)(2,1)} %bitcast.57), custom_call_target="tpu_custom_call" | custom-call | tf_op jit(solution)/shard_map/parcels/pallas_call | solution.py:336
  24.6 7.9 %collective-permute-done.1 = bf16[17,4,8192]{2,1,0:T(4,128)(2,1)S(1)} collective-permute-done((bf16[17,4,8192]{2,1,0:T(4,128)(2,1)S(1)}, bf16[17,4,8192]{2,1,0:T(4,128)(2,1)S(1)}, u32[]{:S(2)}, u32[]{:S(2)}) %collective-permute-start.1) | collective-permute-done | bytes 1114144 | tf_op jit(solution)/shard_map/ppermute | solution.py:77
  35.4 1.3 collective-permute-start.3
  36.7 1.2 broadcast_multiply_fusion.1.refs_4_
  39.8 3.0 %collective-permute-start.5 = (s32[1,1]{1,0:T(1,128)}, s32[1,1]{1,0:T(1,128)}, u32[]{:S(2)}, u32[]{:S(2)}) collective-permute-start(s32[1,1]{1,0:T(1,128)} %max.6), channel_id=1, source_target_pairs={{0,16},{16,0},{1,17},{17,1},{2,18},{18,2},{3,19},{19,3},{4,20},{20... | collective-permute-start | bytes 20 | tf_op jit(solution)/shard_map/ppermute | solution.py:686
  44.1 1.4 fusion.8
  45.5 3.1 %constant_dynamic-slice_fusion.1 = bf16[4096,256]{1,0:T(8,128)(2,1)} fusion(bf16[8192,256]{1,0:T(8,128)(2,1)} %refs_15_.1, s32[]{:T(128)S(6)} %select_n.121), kind=kLoop, calls=%fused_computation.39 | loop fusion | bytes 4194308 | tf_op jit(solution)/shard_map/dynamic_slice | solution.py:87
  48.6 1.7 collective-permute-start.7
  50.3 15.9 %collective-permute-done.3 = bf16[17,4,8192]{2,1,0:T(4,128)(2,1)} collective-permute-done((bf16[17,4,8192]{2,1,0:T(4,128)(2,1)}, bf16[17,4,8192]{2,1,0:T(4,128)(2,1)}, u32[]{:S(2)}, u32[]{:S(2)}) %collective-permute-start.3) | collective-permute-done | bytes 1114144 | tf_op jit(solution)/shard_map/ppermute | solution.py:77
  66.2 1.6 broadcast_select_fusion
  67.7 1.3 collective-permute-start.6
  70.3 54.3 %conditional.1 = (bf16[8,800,256]{2,1,0:T(8,128)(2,1)}) conditional(s32[]{:T(128)} %clamp.3, () %tuple.55, bf16[8,50,16,256]{3,2,1,0:T(8,128)(2,1)} %get-tuple-element.108, bf16[8,50,16,256]{3,2,1,0:T(8,128)(2,1)} %get-tuple-element.108, bf16[8,50,16,256]{3,2,1,0:T(8,128)(2,1)} %get-tuple-element.108, ...), branch_computations={%region_3.4_spmd, %region_4.5_spmd, %region_5.6_spmd, %region_6.7_... | conditional | bytes 19791906 | solution.py:739
  70.4 1.4 slice-done.4
  71.8 50.8 %all_to_all.77 = bf16[8,416,256]{2,1,0:T(8,128)(2,1)S(1)} all-to-all(bf16[8,416,256]{2,1,0:T(8,128)(2,1)S(1)} %bitcast.50), channel_id=1, replica_groups=mesh['groups'=2,'tensor'=8,'section'=2] {'tensor'}, dimensions={0} | all-to-all | bytes 3407872 | tf_op jit(solution)/shard_map/cond/branch_5_fun/all_to_all | solution.py:724
  122.7 1.9 pad.42
  125.3 3.7 %all-to-all-start.12 = ((bf16[8,240,256]{2,1,0:T(8,128)(2,1)}), bf16[8,240,256]{2,1,0:T(8,128)(2,1)S(1)}, u32[]{:S(2)}, u32[]{:S(2)}) async-start(bf16[8,240,256]{2,1,0:T(8,128)(2,1)} %bitcast.59), calls=%async_computation.12 | async-start | bytes 1966080 | tf_op jit(solution)/shard_map/all_to_all | solution.py:724
  129.1 3.9 %select_select_fusion.1 = (bf16[17,4,8192]{2,1,0:T(4,128)(2,1)S(1)}, bf16[17,4,8192]{2,1,0:T(4,128)(2,1)S(1)}, bf16[17,4,8192]{2,1,0:T(4,128)(2,1)S(1)}) fusion(bf16[17,4,8192]{2,1,0:T(4,128)(2,1)} %collective-permute-done.6, bf16[17,4,8192]{2,1,0:T(4,128)(2,1)} %collective-permute-done.3, bf16[17,4,8192]{2,1,0:T(4,128)(2,1)} %copy-done.18, pred[]{:T(512)S(6)} %eq.57, ...), kind=kLoop, calls=%fused_computation.3 | loop fusion | flops 5013504 | bytes 8912899 | tf_op jit(solution)/shard_map/jit(_where)/select_n | solution.py:80
  133.3 6.2 %project.1 = (bf16[256,256]{1,0:T(8,128)(2,1)}, bf16[256,256]{1,0:T(8,128)(2,1)S(1)}, bf16[4,4,8192]{2,1,0:T(4,128)(2,1)S(1)}) custom-call(bf16[17,4,8192]{2,1,0:T(4,128)(2,1)S(1)} %copy-done.4, bf16[17,4,8192]{2,1,0:T(4,128)(2,1)S(1)} %get-tuple-element.157.refs_1_, bf16[17,4,8192]{2,1,0:T(4,128)(2,1)S(1)} %get-tuple-element.156.refs_2_, ...), custom_call_target="tpu_custom_call" | custom-call | flops 2147483648 | bytes 8388608 | tf_op jit(solution)/shard_map/project/pallas_call | solution.py:272
  139.5 1.7 collective-permute-start.11
  141.8 7.1 %collective-permute-done.11 = bf16[256,256]{1,0:T(8,128)(2,1)S(1)} collective-permute-done((bf16[256,256]{1,0:T(8,128)(2,1)S(1)}, bf16[256,256]{1,0:T(8,128)(2,1)S(1)}, u32[]{:S(2)}, u32[]{:S(2)}) %collective-permute-start.11) | collective-permute-done | bytes 131104 | tf_op jit(solution)/shard_map/ppermute | solution.py:61
  148.9 5.4 %collective-permute-done.9.refs_1_ = bf16[4,4,8192]{2,1,0:T(4,128)(2,1)S(1)} collective-permute-done((bf16[4,4,8192]{2,1,0:T(4,128)(2,1)S(1)}, bf16[4,4,8192]{2,1,0:T(4,128)(2,1)S(1)}, u32[]{:S(2)}, u32[]{:S(2)}) %collective-permute-start.9) | collective-permute-done | bytes 262176 | tf_op jit(solution)/shard_map/ppermute | solution.py:61
  156.2 12.4 %decode_step.4 = (bf16[8,4,8192]{2,1,0:T(4,128)(2,1)S(1)}, bf16[32,256]{1,0:T(8,128)(2,1)S(1)}, bf16[8192,512]{1,0:T(8,128)(2,1)S(1)}, bf16[8192,256]{1,0:T(8,12...) custom-call(bf16[4,4,8192]{2,1,0:T(4,128)(2,1)S(1)} %get-tuple-element.121.refs_0_, ...), custom_call_target="tpu_custom_call" | custom-call | flops 671088640 | bytes 25231360 | tf_op jit(solution)/shard_map/decode_step/pallas_call | solution.py:578
  168.7 18.9 %all_to_all.85.parts_ref = bf16[8,4,8192]{2,1,0:T(4,128)(2,1)S(1)} all-to-all(bf16[8,4,8192]{2,1,0:T(4,128)(2,1)S(1)} %get-tuple-element.131), channel_id=1, replica_groups=mesh['groups'=2,'tensor'=8,'section'=2] {'tensor'}, dimensions={0} | all-to-all | bytes 1048576 | tf_op jit(solution)/shard_map/all_to_all | solution.py:778
  187.9 1.2 collective-permute-start.16
  189.7 2.6 collective-permute-start.14
  192.3 1.5 collective-permute-start.13
  195.9 1.7 collective-permute-start.17
  200.1 6.2 %decode_step.5 = (bf16[8,4,8192]{2,1,0:T(4,128)(2,1)S(1)}, bf16[32,256]{1,0:T(8,128)(2,1)S(1)}) custom-call(bf16[4,8192]{1,0:T(4,128)(2,1)S(1)} %get-tuple-element.134.refs_0_, bf16[4,8192]{1,0:T(4,128)(2,1)S(1)} %collective-permute-done.13.refs_1_, bf16[4,8192]{1,0:T(4,128)(2,1)S(1)} %collective-permute-done.14.refs_2_, ...), custom_call_target="tpu_custom_call" | custom-call | flops 671088640 | bytes 25231360 | tf_op jit(solution)/shard_map/decode_step/pallas_call | solution.py:578
  206.3 15.9 %all_to_all.86.parts_ref = bf16[8,4,8192]{2,1,0:T(4,128)(2,1)S(1)} all-to-all(bf16[8,4,8192]{2,1,0:T(4,128)(2,1)S(1)} %get-tuple-element.141), channel_id=1, replica_groups=mesh['groups'=2,'tensor'=8,'section'=2] {'tensor'}, dimensions={0} | all-to-all | bytes 1048576 | tf_op jit(solution)/shard_map/all_to_all | solution.py:778
  224.4 2.5 collective-permute-start.21
  227.0 1.5 collective-permute-start.20
  228.4 1.3 collective-permute-start.26
  230.6 1.5 collective-permute-start.24
  232.7 1.3 collective-permute-done.25.refs_6_
  234.9 6.2 %decode_step.6 = (bf16[8,4,8192]{2,1,0:T(4,128)(2,1)S(1)}, bf16[32,256]{1,0:T(8,128)(2,1)S(1)}) custom-call(bf16[4,8192]{1,0:T(4,128)(2,1)S(1)} %get-tuple-element.143.refs_0_, bf16[4,8192]{1,0:T(4,128)(2,1)S(1)} %collective-permute-done.20.refs_1_, bf16[4,8192]{1,0:T(4,128)(2,1)S(1)} %collective-permute-done.21.refs_2_, ...), custom_call_target="tpu_custom_call" | custom-call | flops 671088640 | bytes 25231360 | tf_op jit(solution)/shard_map/decode_step/pallas_call | solution.py:578
  241.1 16.5 %all_to_all.87.parts_ref = bf16[8,4,8192]{2,1,0:T(4,128)(2,1)S(1)} all-to-all(bf16[8,4,8192]{2,1,0:T(4,128)(2,1)S(1)} %get-tuple-element.145), channel_id=1, replica_groups=mesh['groups'=2,'tensor'=8,'section'=2] {'tensor'}, dimensions={0} | all-to-all | bytes 1048576 | tf_op jit(solution)/shard_map/all_to_all | solution.py:778
  258.3 2.3 collective-permute-start.29
  260.6 1.7 collective-permute-start.28
  262.3 1.6 collective-permute-start.27
  264.4 1.6 collective-permute-start.32
  266.7 1.8 collective-permute-start.31
  268.9 2.1 collective-permute-done.31.refs_5_
  270.9 6.2 %decode_step.7 = (bf16[8,4,8192]{2,1,0:T(4,128)(2,1)S(1)}, bf16[32,256]{1,0:T(8,128)(2,1)}) custom-call(bf16[4,8192]{1,0:T(4,128)(2,1)S(1)} %get-tuple-element.147.refs_0_, bf16[4,8192]{1,0:T(4,128)(2,1)S(1)} %collective-permute-done.27.refs_1_, bf16[4,8192]{1,0:T(4,128)(2,1)S(1)} %collective-permute-done.28.refs_2_, ...), custom_call_target="tpu_custom_call" | custom-call | flops 671088640 | bytes 25231360 | tf_op jit(solution)/shard_map/decode_step/pallas_call | solution.py:578
  277.2 14.1 %all_to_all.88.parts_ref = bf16[8,4,8192]{2,1,0:T(4,128)(2,1)S(1)} all-to-all(bf16[8,4,8192]{2,1,0:T(4,128)(2,1)S(1)} %get-tuple-element.149), channel_id=1, replica_groups=mesh['groups'=2,'tensor'=8,'section'=2] {'tensor'}, dimensions={0} | all-to-all | bytes 1048576 | tf_op jit(solution)/shard_map/all_to_all | solution.py:778
  (131 shorter events, 29.6 us)
Async XLA Ops:
  0.0 69.0 %copy-start = (s32[2,4,8]{2,1,0:T(4,128)S(1)}, s32[2,4,8]{2,1,0:T(4,128)}, u32[]{:S(2)}) copy-start(s32[2,4,8]{2,1,0:T(4,128)} %param.44) | copy-start | bytes 772
  3.0 21.1 %copy-start.3 = (bf16[17,4,8192]{2,1,0:T(4,128)(2,1)}, bf16[17,4,8192]{2,1,0:T(4,128)(2,1)S(1)}, u32[]{:S(2)}) copy-start(bf16[17,4,8192]{2,1,0:T(4,128)(2,1)S(1)} %get-tuple-element.109.refs_0_) | copy-start | bytes 3342340
  3.0 29.5 %collective-permute-start.1 = (bf16[17,4,8192]{2,1,0:T(4,128)(2,1)S(1)}, bf16[17,4,8192]{2,1,0:T(4,128)(2,1)S(1)}, u32[]{:S(2)}, u32[]{:S(2)}) collective-permute-start(bf16[17,4,8192]{2,1,0:T(4,128)(2,1)S(1)} %get-tuple-element.109.refs_0_), channel_id=1, source_target_pairs={{4,0},{6,2},{8,4},{10,6},{12,8},{14,10},{5,1},{7,3},{9,5},{11,7},{... | collective-permute-start | bytes 3342344 | tf_op jit(solution)/shard_map/ppermute | solution.py:77
  4.3 29.4 %collective-permute-start = (bf16[17,4,8192]{2,1,0:T(4,128)(2,1)S(1)}, bf16[17,4,8192]{2,1,0:T(4,128)(2,1)S(1)}, u32[]{:S(2)}, u32[]{:S(2)}) collective-permute-start(bf16[17,4,8192]{2,1,0:T(4,128)(2,1)S(1)} %get-tuple-element.109.refs_0_), channel_id=1, source_target_pairs={{0,4},{2,6},{4,8},{6,10},{8,12},{10,14},{1,5},{3,7},{5,9},{7,11},{... | collective-permute-start | bytes 3342344 | tf_op jit(solution)/shard_map/ppermute | solution.py:77
  11.5 27.0 %collective-permute-start.4 = (s32[1,1]{1,0:T(1,128)}, s32[1,1]{1,0:T(1,128)}, u32[]{:S(2)}, u32[]{:S(2)}) collective-permute-start(s32[1,1]{1,0:T(1,128)} %bitcast.18), channel_id=1, source_target_pairs={{0,1},{1,0},{2,3},{3,2},{4,5},{5,4},{6,7},{7,6},{8,9},{9,8},{10,11... | collective-permute-start | bytes 20 | tf_op jit(solution)/shard_map/ppermute | solution.py:686
  18.4 5.7 %copy-start.10 = (s32[1,32]{1,0:T(1,128)S(1)}, s32[1,32]{1,0:T(1,128)}, u32[]{:S(2)}) copy-start(s32[1,32]{1,0:T(1,128)} %param.42) | copy-start | bytes 388
  18.4 6.1 %copy-start.22 = (s32[32]{0:T(128)S(1)}, s32[32]{0:T(128)}, u32[]{:S(2)}) copy-start(s32[32]{0:T(128)} %reshape.179) | copy-start | bytes 388
  18.5 6.1 %copy-start.23 = (s32[32]{0:T(128)S(1)}, s32[32]{0:T(128)}, u32[]{:S(2)}) copy-start(s32[32]{0:T(128)} %reshape.180) | copy-start | bytes 388
  34.7 15.6 %collective-permute-start.2 = (bf16[17,4,8192]{2,1,0:T(4,128)(2,1)}, bf16[17,4,8192]{2,1,0:T(4,128)(2,1)S(1)}, u32[]{:S(2)}, u32[]{:S(2)}) collective-permute-start(bf16[17,4,8192]{2,1,0:T(4,128)(2,1)} %copy-done.20), channel_id=1, source_target_pairs={{4,8},{6,10},{8,12},{10,14},{5,9},{7,11},{9,13},{11,15},{20,24},{2... | collective-permute-start | bytes 3342344 | tf_op jit(solution)/shard_map/ppermute | solution.py:77
  35.4 30.8 %collective-permute-start.3 = (bf16[17,4,8192]{2,1,0:T(4,128)(2,1)}, bf16[17,4,8192]{2,1,0:T(4,128)(2,1)}, u32[]{:S(2)}, u32[]{:S(2)}) collective-permute-start(bf16[17,4,8192]{2,1,0:T(4,128)(2,1)} %copy-done.19), channel_id=1, source_target_pairs={{4,0},{6,2},{8,4},{10,6},{5,1},{7,3},{9,5},{11,7},{20,16},{22,18},... | collective-permute-start | bytes 3342344 | tf_op jit(solution)/shard_map/ppermute | solution.py:77
  39.8 3.6 %collective-permute-start.5 = (s32[1,1]{1,0:T(1,128)}, s32[1,1]{1,0:T(1,128)}, u32[]{:S(2)}, u32[]{:S(2)}) collective-permute-start(s32[1,1]{1,0:T(1,128)} %max.6), channel_id=1, source_target_pairs={{0,16},{16,0},{1,17},{17,1},{2,18},{18,2},{3,19},{19,3},{4,20},{20... | collective-permute-start | bytes 20 | tf_op jit(solution)/shard_map/ppermute | solution.py:686
  48.6 76.1 %collective-permute-start.7 = (bf16[4096,256]{1,0:T(8,128)(2,1)}, bf16[4096,256]{1,0:T(8,128)(2,1)S(1)}, u32[]{:S(2)}, u32[]{:S(2)}) collective-permute-start(bf16[4096,256]{1,0:T(8,128)(2,1)} %constant_dynamic-slice_fusion.1), channel_id=1, source_target_pairs={{0,2},{2,0},{4,6},{6,4},{8,10},{10,8},{12,14},{14,12},{1,3},{3,1},... | collective-permute-start | bytes 6291464 | tf_op jit(solution)/shard_map/ppermute | solution.py:61
  50.3 20.1 %copy-start.18 = (bf16[17,4,8192]{2,1,0:T(4,128)(2,1)}, bf16[17,4,8192]{2,1,0:T(4,128)(2,1)S(1)}, u32[]{:S(2)}) copy-start(bf16[17,4,8192]{2,1,0:T(4,128)(2,1)S(1)} %collective-permute-done.2) | copy-start | bytes 3342340
  67.7 56.9 %collective-permute-start.6 = (bf16[17,4,8192]{2,1,0:T(4,128)(2,1)}, bf16[17,4,8192]{2,1,0:T(4,128)(2,1)}, u32[]{:S(2)}, u32[]{:S(2)}) collective-permute-start(bf16[17,4,8192]{2,1,0:T(4,128)(2,1)} %broadcast_select_fusion), channel_id=1, source_target_pairs={{4,0},{6,2},{8,12},{10,14},{5,1},{7,3},{9,13},{11,15},{20,16},{22,... | collective-permute-start | bytes 3342344 | tf_op jit(solution)/shard_map/ppermute | solution.py:92
  124.6 8.4 %collective-permute-start.8 = (bf16[4096,256]{1,0:T(8,128)(2,1)S(1)}, bf16[4096,256]{1,0:T(8,128)(2,1)}, u32[]{:S(2)}, u32[]{:S(2)}) collective-permute-start(bf16[4096,256]{1,0:T(8,128)(2,1)S(1)} %collective-permute-done.7.refs_9_), channel_id=1, source_target_pairs={{0,1},{1,0},{2,3},{3,2},{4,5},{5,4},{6,7},{7,6},{8,9},{9,8},{10,11... | collective-permute-start | bytes 6291464 | tf_op jit(solution)/shard_map/ppermute | solution.py:96
  125.3 29.0 %all-to-all-start.12 = ((bf16[8,240,256]{2,1,0:T(8,128)(2,1)}), bf16[8,240,256]{2,1,0:T(8,128)(2,1)S(1)}, u32[]{:S(2)}, u32[]{:S(2)}) async-start(bf16[8,240,256]{2,1,0:T(8,128)(2,1)} %bitcast.59), calls=%async_computation.12 | async-start | bytes 1966080 | tf_op jit(solution)/shard_map/all_to_all | solution.py:724
  129.1 4.2 %copy-start.4 = (bf16[17,4,8192]{2,1,0:T(4,128)(2,1)S(1)}, bf16[17,4,8192]{2,1,0:T(4,128)(2,1)}, u32[]{:S(2)}) copy-start(bf16[17,4,8192]{2,1,0:T(4,128)(2,1)} %copy-done.3) | copy-start | bytes 3342340
  129.1 4.2 %copy-start.5 = (f32[128,128]{1,0:T(8,128)S(1)}, f32[128,128]{1,0:T(8,128)}, u32[]{:S(2)}) copy-start(f32[128,128]{1,0:T(8,128)} %constant.217.clone.refs_7_) | copy-start | bytes 196612
  133.2 8.0 %copy-start.21 = (s32[4,8]{1,0:T(4,128)S(1)}, s32[4,8]{1,0:T(4,128)}, u32[]{:S(2)}) copy-start(s32[4,8]{1,0:T(4,128)} %dynamic-slice_bitcast_fusion) | copy-start | bytes 388
  133.3 8.4 %copy-start.24 = (s32[2,4]{1,0:T(2,128)S(1)}, s32[2,4]{1,0:T(2,128)}, u32[]{:S(2)}) copy-start(s32[2,4]{1,0:T(2,128)} %param.43) | copy-start | bytes 100
  133.3 8.4 %copy-start.8 = (bf16[8192]{0:T(1024)(128)(2,1)S(1)}, bf16[8192]{0:T(1024)(128)(2,1)}, u32[]{:S(2)}) copy-start(bf16[8192]{0:T(1024)(128)(2,1)} %param.36) | copy-start | bytes 49156
  139.5 9.4 %collective-permute-start.11 = (bf16[256,256]{1,0:T(8,128)(2,1)S(1)}, bf16[256,256]{1,0:T(8,128)(2,1)S(1)}, u32[]{:S(2)}, u32[]{:S(2)}) collective-permute-start(bf16[256,256]{1,0:T(8,128)(2,1)S(1)} %get-tuple-element.127), channel_id=1, source_target_pairs={{0,2},{2,0},{4,6},{6,4},{8,10},{10,8},{12,14},{14,12},{1,3},{3,1},... | collective-permute-start | bytes 393224 | tf_op jit(solution)/shard_map/ppermute | solution.py:61
  141.3 12.9 %collective-permute-start.9 = (bf16[4,4,8192]{2,1,0:T(4,128)(2,1)S(1)}, bf16[4,4,8192]{2,1,0:T(4,128)(2,1)S(1)}, u32[]{:S(2)}, u32[]{:S(2)}) collective-permute-start(bf16[4,4,8192]{2,1,0:T(4,128)(2,1)S(1)} %get-tuple-element.121.refs_0_), channel_id=1, source_target_pairs={{0,2},{2,0},{4,6},{6,4},{8,10},{10,8},{12,14},{14,12},{1,3},{3,1},... | collective-permute-start | bytes 786440 | tf_op jit(solution)/shard_map/ppermute | solution.py:61
  141.7 12.5 %collective-permute-start.10 = (bf16[256,256]{1,0:T(8,128)(2,1)}, bf16[256,256]{1,0:T(8,128)(2,1)S(1)}, u32[]{:S(2)}, u32[]{:S(2)}) collective-permute-start(bf16[256,256]{1,0:T(8,128)(2,1)} %get-tuple-element.126), channel_id=1, source_target_pairs={{0,1},{1,0},{2,3},{3,2},{4,5},{5,4},{6,7},{7,6},{8,9},{9,8},{10,11... | collective-permute-start | bytes 393224 | tf_op jit(solution)/shard_map/ppermute | solution.py:760
  148.9 5.4 %collective-permute-start.12 = (bf16[256,256]{1,0:T(8,128)(2,1)S(1)}, bf16[256,256]{1,0:T(8,128)(2,1)S(1)}, u32[]{:S(2)}, u32[]{:S(2)}) collective-permute-start(bf16[256,256]{1,0:T(8,128)(2,1)S(1)} %collective-permute-done.11), channel_id=1, source_target_pairs={{0,1},{1,0},{2,3},{3,2},{4,5},{5,4},{6,7},{7,6},{8,9},{9,8},{10,11... | collective-permute-start | bytes 393224 | tf_op jit(solution)/shard_map/ppermute | solution.py:760
  187.9 6.0 %collective-permute-start.16 = (bf16[4,8192]{1,0:T(4,128)(2,1)S(1)}, bf16[4,8192]{1,0:T(4,128)(2,1)S(1)}, u32[]{:S(2)}, u32[]{:S(2)}) collective-permute-start(bf16[4,8192]{1,0:T(4,128)(2,1)S(1)} %get-tuple-element.134.refs_0_), channel_id=1, source_target_pairs={{0,4},{2,6},{4,0},{6,2},{8,12},{10,14},{12,8},{14,10},{1,5},{3,7},... | collective-permute-start | bytes 196616 | tf_op jit(solution)/shard_map/ppermute | solution.py:31
  189.1 5.9 %collective-permute-start.15 = (bf16[4,8192]{1,0:T(4,128)(2,1)S(1)}, bf16[4,8192]{1,0:T(4,128)(2,1)S(1)}, u32[]{:S(2)}, u32[]{:S(2)}) collective-permute-start(bf16[4,8192]{1,0:T(4,128)(2,1)S(1)} %get-tuple-element.134.refs_0_), channel_id=1, source_target_pairs={{0,8},{2,10},{4,12},{6,14},{8,0},{10,2},{12,4},{14,6},{1,9},{3,11}... | collective-permute-start | bytes 196616 | tf_op jit(solution)/shard_map/ppermute | solution.py:31
  189.7 6.2 %collective-permute-start.14 = (bf16[4,8192]{1,0:T(4,128)(2,1)S(1)}, bf16[4,8192]{1,0:T(4,128)(2,1)S(1)}, u32[]{:S(2)}, u32[]{:S(2)}) collective-permute-start(bf16[4,8192]{1,0:T(4,128)(2,1)S(1)} %get-tuple-element.134.refs_0_), channel_id=1, source_target_pairs={{0,12},{2,14},{4,8},{6,10},{8,4},{10,6},{12,0},{14,2},{1,13},{3,15... | collective-permute-start | bytes 196616 | tf_op jit(solution)/shard_map/ppermute | solution.py:31
  192.3 5.3 %collective-permute-start.13 = (bf16[4,8192]{1,0:T(4,128)(2,1)S(1)}, bf16[4,8192]{1,0:T(4,128)(2,1)S(1)}, u32[]{:S(2)}, u32[]{:S(2)}) collective-permute-start(bf16[4,8192]{1,0:T(4,128)(2,1)S(1)} %get-tuple-element.134.refs_0_), channel_id=1, source_target_pairs={{0,2},{2,0},{4,6},{6,4},{8,10},{10,8},{12,14},{14,12},{1,3},{3,1},... | collective-permute-start | bytes 196616 | tf_op jit(solution)/shard_map/ppermute | solution.py:61
  193.8 4.3 %collective-permute-start.19 = (bf16[4,8192]{1,0:T(4,128)(2,1)S(1)}, bf16[4,8192]{1,0:T(4,128)(2,1)S(1)}, u32[]{:S(2)}, u32[]{:S(2)}) collective-permute-start(bf16[4,8192]{1,0:T(4,128)(2,1)S(1)} %collective-permute-done.16.refs_4_), channel_id=1, source_target_pairs={{0,2},{2,0},{4,6},{6,4},{8,10},{10,8},{12,14},{14,12},{1,3},{3,1},... | collective-permute-start | bytes 196616 | tf_op jit(solution)/shard_map/ppermute | solution.py:61
  195.0 4.3 %collective-permute-start.18 = (bf16[4,8192]{1,0:T(4,128)(2,1)S(1)}, bf16[4,8192]{1,0:T(4,128)(2,1)S(1)}, u32[]{:S(2)}, u32[]{:S(2)}) collective-permute-start(bf16[4,8192]{1,0:T(4,128)(2,1)S(1)} %collective-permute-done.15.refs_3_), channel_id=1, source_target_pairs={{0,2},{2,0},{4,6},{6,4},{8,10},{10,8},{12,14},{14,12},{1,3},{3,1},... | collective-permute-start | bytes 196616 | tf_op jit(solution)/shard_map/ppermute | solution.py:61
  195.9 4.3 %collective-permute-start.17 = (bf16[4,8192]{1,0:T(4,128)(2,1)S(1)}, bf16[4,8192]{1,0:T(4,128)(2,1)S(1)}, u32[]{:S(2)}, u32[]{:S(2)}) collective-permute-start(bf16[4,8192]{1,0:T(4,128)(2,1)S(1)} %collective-permute-done.14.refs_2_), channel_id=1, source_target_pairs={{0,2},{2,0},{4,6},{6,4},{8,10},{10,8},{12,14},{14,12},{1,3},{3,1},... | collective-permute-start | bytes 196616 | tf_op jit(solution)/shard_map/ppermute | solution.py:61
  222.5 5.9 %collective-permute-start.23 = (bf16[4,8192]{1,0:T(4,128)(2,1)S(1)}, bf16[4,8192]{1,0:T(4,128)(2,1)S(1)}, u32[]{:S(2)}, u32[]{:S(2)}) collective-permute-start(bf16[4,8192]{1,0:T(4,128)(2,1)S(1)} %get-tuple-element.143.refs_0_), channel_id=1, source_target_pairs={{0,4},{2,6},{4,0},{6,2},{8,12},{10,14},{12,8},{14,10},{1,5},{3,7},... | collective-permute-start | bytes 196616 | tf_op jit(solution)/shard_map/ppermute | solution.py:31
  223.7 6.0 %collective-permute-start.22 = (bf16[4,8192]{1,0:T(4,128)(2,1)S(1)}, bf16[4,8192]{1,0:T(4,128)(2,1)S(1)}, u32[]{:S(2)}, u32[]{:S(2)}) collective-permute-start(bf16[4,8192]{1,0:T(4,128)(2,1)S(1)} %get-tuple-element.143.refs_0_), channel_id=1, source_target_pairs={{0,8},{2,10},{4,12},{6,14},{8,0},{10,2},{12,4},{14,6},{1,9},{3,11}... | collective-permute-start | bytes 196616 | tf_op jit(solution)/shard_map/ppermute | solution.py:31
  224.4 6.2 %collective-permute-start.21 = (bf16[4,8192]{1,0:T(4,128)(2,1)S(1)}, bf16[4,8192]{1,0:T(4,128)(2,1)S(1)}, u32[]{:S(2)}, u32[]{:S(2)}) collective-permute-start(bf16[4,8192]{1,0:T(4,128)(2,1)S(1)} %get-tuple-element.143.refs_0_), channel_id=1, source_target_pairs={{0,12},{2,14},{4,8},{6,10},{8,4},{10,6},{12,0},{14,2},{1,13},{3,15... | collective-permute-start | bytes 196616 | tf_op jit(solution)/shard_map/ppermute | solution.py:31
  227.0 5.2 %collective-permute-start.20 = (bf16[4,8192]{1,0:T(4,128)(2,1)S(1)}, bf16[4,8192]{1,0:T(4,128)(2,1)S(1)}, u32[]{:S(2)}, u32[]{:S(2)}) collective-permute-start(bf16[4,8192]{1,0:T(4,128)(2,1)S(1)} %get-tuple-element.143.refs_0_), channel_id=1, source_target_pairs={{0,2},{2,0},{4,6},{6,4},{8,10},{10,8},{12,14},{14,12},{1,3},{3,1},... | collective-permute-start | bytes 196616 | tf_op jit(solution)/shard_map/ppermute | solution.py:61
  228.4 4.3 %collective-permute-start.26 = (bf16[4,8192]{1,0:T(4,128)(2,1)S(1)}, bf16[4,8192]{1,0:T(4,128)(2,1)S(1)}, u32[]{:S(2)}, u32[]{:S(2)}) collective-permute-start(bf16[4,8192]{1,0:T(4,128)(2,1)S(1)} %collective-permute-done.23.refs_4_), channel_id=1, source_target_pairs={{0,2},{2,0},{4,6},{6,4},{8,10},{10,8},{12,14},{14,12},{1,3},{3,1},... | collective-permute-start | bytes 196616 | tf_op jit(solution)/shard_map/ppermute | solution.py:61
  229.7 4.3 %collective-permute-start.25 = (bf16[4,8192]{1,0:T(4,128)(2,1)S(1)}, bf16[4,8192]{1,0:T(4,128)(2,1)S(1)}, u32[]{:S(2)}, u32[]{:S(2)}) collective-permute-start(bf16[4,8192]{1,0:T(4,128)(2,1)S(1)} %collective-permute-done.22.refs_3_), channel_id=1, source_target_pairs={{0,2},{2,0},{4,6},{6,4},{8,10},{10,8},{12,14},{14,12},{1,3},{3,1},... | collective-permute-start | bytes 196616 | tf_op jit(solution)/shard_map/ppermute | solution.py:61
  230.6 4.3 %collective-permute-start.24 = (bf16[4,8192]{1,0:T(4,128)(2,1)S(1)}, bf16[4,8192]{1,0:T(4,128)(2,1)S(1)}, u32[]{:S(2)}, u32[]{:S(2)}) collective-permute-start(bf16[4,8192]{1,0:T(4,128)(2,1)S(1)} %collective-permute-done.21.refs_2_), channel_id=1, source_target_pairs={{0,2},{2,0},{4,6},{6,4},{8,10},{10,8},{12,14},{14,12},{1,3},{3,1},... | collective-permute-start | bytes 196616 | tf_op jit(solution)/shard_map/ppermute | solution.py:61
  234.9 36.1 %copy-start.12 = (s32[32]{0:T(128)S(1)}, s32[32]{0:T(128)}, u32[]{:S(2)}) copy-start(s32[32]{0:T(128)} %get-tuple-element.151.refs_5_.refs_11_) | copy-start | bytes 388
  257.9 6.0 %collective-permute-start.30 = (bf16[4,8192]{1,0:T(4,128)(2,1)S(1)}, bf16[4,8192]{1,0:T(4,128)(2,1)S(1)}, u32[]{:S(2)}, u32[]{:S(2)}) collective-permute-start(bf16[4,8192]{1,0:T(4,128)(2,1)S(1)} %get-tuple-element.147.refs_0_), channel_id=1, source_target_pairs={{0,4},{2,6},{4,0},{6,2},{8,12},{10,14},{12,8},{14,10},{1,5},{3,7},... | collective-permute-start | bytes 196616 | tf_op jit(solution)/shard_map/ppermute | solution.py:31
  258.3 6.1 %collective-permute-start.29 = (bf16[4,8192]{1,0:T(4,128)(2,1)S(1)}, bf16[4,8192]{1,0:T(4,128)(2,1)S(1)}, u32[]{:S(2)}, u32[]{:S(2)}) collective-permute-start(bf16[4,8192]{1,0:T(4,128)(2,1)S(1)} %get-tuple-element.147.refs_0_), channel_id=1, source_target_pairs={{0,8},{2,10},{4,12},{6,14},{8,0},{10,2},{12,4},{14,6},{1,9},{3,11}... | collective-permute-start | bytes 196616 | tf_op jit(solution)/shard_map/ppermute | solution.py:31
  260.6 6.1 %collective-permute-start.28 = (bf16[4,8192]{1,0:T(4,128)(2,1)S(1)}, bf16[4,8192]{1,0:T(4,128)(2,1)S(1)}, u32[]{:S(2)}, u32[]{:S(2)}) collective-permute-start(bf16[4,8192]{1,0:T(4,128)(2,1)S(1)} %get-tuple-element.147.refs_0_), channel_id=1, source_target_pairs={{0,12},{2,14},{4,8},{6,10},{8,4},{10,6},{12,0},{14,2},{1,13},{3,15... | collective-permute-start | bytes 196616 | tf_op jit(solution)/shard_map/ppermute | solution.py:31
  262.3 6.1 %collective-permute-start.27 = (bf16[4,8192]{1,0:T(4,128)(2,1)S(1)}, bf16[4,8192]{1,0:T(4,128)(2,1)S(1)}, u32[]{:S(2)}, u32[]{:S(2)}) collective-permute-start(bf16[4,8192]{1,0:T(4,128)(2,1)S(1)} %get-tuple-element.147.refs_0_), channel_id=1, source_target_pairs={{0,2},{2,0},{4,6},{6,4},{8,10},{10,8},{12,14},{14,12},{1,3},{3,1},... | collective-permute-start | bytes 196616 | tf_op jit(solution)/shard_map/ppermute | solution.py:61
  263.9 4.6 %collective-permute-start.33 = (bf16[4,8192]{1,0:T(4,128)(2,1)S(1)}, bf16[4,8192]{1,0:T(4,128)(2,1)S(1)}, u32[]{:S(2)}, u32[]{:S(2)}) collective-permute-start(bf16[4,8192]{1,0:T(4,128)(2,1)S(1)} %collective-permute-done.30.refs_4_), channel_id=1, source_target_pairs={{0,2},{2,0},{4,6},{6,4},{8,10},{10,8},{12,14},{14,12},{1,3},{3,1},... | collective-permute-start | bytes 196616 | tf_op jit(solution)/shard_map/ppermute | solution.py:61
  264.4 4.5 %collective-permute-start.32 = (bf16[4,8192]{1,0:T(4,128)(2,1)S(1)}, bf16[4,8192]{1,0:T(4,128)(2,1)S(1)}, u32[]{:S(2)}, u32[]{:S(2)}) collective-permute-start(bf16[4,8192]{1,0:T(4,128)(2,1)S(1)} %collective-permute-done.29.refs_3_), channel_id=1, source_target_pairs={{0,2},{2,0},{4,6},{6,4},{8,10},{10,8},{12,14},{14,12},{1,3},{3,1},... | collective-permute-start | bytes 196616 | tf_op jit(solution)/shard_map/ppermute | solution.py:61
  266.7 4.3 %collective-permute-start.31 = (bf16[4,8192]{1,0:T(4,128)(2,1)S(1)}, bf16[4,8192]{1,0:T(4,128)(2,1)S(1)}, u32[]{:S(2)}, u32[]{:S(2)}) collective-permute-start(bf16[4,8192]{1,0:T(4,128)(2,1)S(1)} %collective-permute-done.28.refs_2_), channel_id=1, source_target_pairs={{0,2},{2,0},{4,6},{6,4},{8,10},{10,8},{12,14},{14,12},{1,3},{3,1},... | collective-permute-start | bytes 196616 | tf_op jit(solution)/shard_map/ppermute | solution.py:61
  270.9 21.2 %copy-start.1 = (s32[2,4,8]{2,1,0:T(4,128)S(1)}, s32[2,4,8]{2,1,0:T(4,128)}, u32[]{:S(2)}) copy-start(s32[2,4,8]{2,1,0:T(4,128)} %param.44) | copy-start | bytes 772
  (13 other events, 23.9 us)
